TPU v7x, 32 devices: a whole 2x2x4 slice. The times are simulated.
32 devices in a mesh: parts: 2 (over x), tm: 16 (over z, y, core).
Axes of the slice: x: 2, y: 2, z: 4, core: 2. Of those that a mesh axis runs over, the one named last changes fastest.
Arguments:
- observed: float32 [64, 128], P(('parts', 'tm')), parts along dimension 0, may hold values from -6 to 6
- obs_mask: int32 [64, 128], P(('parts', 'tm')), parts along dimension 0, may hold values 0 or 1
- prior_mean: float32 [256], P('parts'), parts along dimension 0, may hold values from -6 to 6
- prior_var: float32 [256], P('parts'), parts along dimension 0, may hold values from 0.5 to 2
- neighbor_weights: float32 [8, 128], replicated, may hold values from 0.01 to 0.06
- damping: float32 [128], replicated, may hold values from 0.0005 to 0.005
- process_var: float32 [128], replicated, may hold values from 0.0005 to 0.002
- obs_var: float32 [128], replicated, may hold values from 1 to 4
Outputs:
- smoothed_mean: float32 [64, 128], P(('parts', 'tm')), parts along dimension 0
- smoothed_cov: float32 [64, 128, 128], P(('parts', 'tm')), parts along dimension 0
- loglik: float32 [64], P(('parts', 'tm')), parts along dimension 0
There are 2 independent parts, one for each index of `parts`. A program takes and returns all parts, laid end to end along the dimension named above; an argument that names none is the same for every part. Nothing has to cross between parts.
Inputs may be any that keep to these rules, and one draw needn't show every extreme that they name: `obs_mask`: 1 where a cell is observed at a step, 0 where it is not.
All inputs are finite; a program needn't handle non-finite values. No bound on the sum of `obs_mask` on one device may be relied on, other than what follows from the above.
Results may differ from a plain program's by a relative error of at most 0.0003.
Values sent between devices are 32-bit elements; how exact they have to be, the bound alone decides.
No kernel may reach another device: no remote copies, remote signals or barrier semaphores. Data moves between devices by JAX's collectives and lax.ppermute only.
A program may use at most 128 MiB of HBM per device.

v0:
```python
import math

import jax
import jax.numpy as jnp
from jax import lax
from jax.sharding import PartitionSpec as P

GX = 16
GY = 8


OFFSETS = ((-1, -1), (-1, 0), (-1, 1), (0, -1), (0, 1), (1, -1), (1, 0), (1, 1))
LOG_TWO_PI = math.log(2.0 * math.pi)


def carried_in(array, axis, combine, identity, reverse):
    size, position = (lax.axis_size(axis), lax.axis_index(axis))
    everything = jax.tree.map(lambda part: lax.all_gather(part, axis), array)
    start = jax.tree.map(
        lambda part, zero: jnp.broadcast_to(jnp.asarray(zero, part.dtype), part.shape),
        array,
        identity,
    )

    def lap(k, before):
        at = size - 1 - k if reverse else k
        reached = at > position if reverse else at < position
        new = combine(before, jax.tree.map(lambda part: part[at], everything))
        return jax.tree.map(lambda a, b: jnp.where(reached, a, b), new, before)

    return lax.fori_loop(0, size, lap, start)


def from_behind(array, axis, by):
    size = lax.axis_size(axis)
    pairs = [(i, i + by) for i in range(size) if 0 <= i + by < size]
    return lax.ppermute(array, axis, pairs)


def high_dot(left, right):
    return jnp.dot(left, right, precision=lax.Precision.HIGHEST, preferred_element_type=jnp.float32)


def tri_solve(lower_mat, rhs):
    return jax.scipy.linalg.solve_triangular(lower_mat, rhs, lower=True)


def advance(matrix_in, neighbor_weights, damping):
    centre = 1.0 - jnp.sum(neighbor_weights, axis=0) - damping
    columns = matrix_in.shape[1]
    gridded = matrix_in.reshape(GX, GY, columns)
    padded = jnp.pad(gridded, ((1, 1), (1, 1), (0, 0)))
    summed = centre.reshape(GX, GY, 1) * gridded
    for offset_index in range(8):
        shift_x, shift_y = OFFSETS[offset_index]
        summed = (
            summed
            + neighbor_weights[offset_index].reshape(GX, GY, 1)
            * padded[1 + shift_x : 1 + shift_x + GX, 1 + shift_y : 1 + shift_y + GY]
        )
    return summed.reshape(GX * GY, columns)


def retreat(matrix_in, neighbor_weights, damping):
    centre = 1.0 - jnp.sum(neighbor_weights, axis=0) - damping
    columns = matrix_in.shape[1]
    gridded = matrix_in.reshape(GX, GY, columns)
    summed = centre.reshape(GX, GY, 1) * gridded
    for offset_index in range(8):
        shift_x, shift_y = OFFSETS[offset_index]
        weighted = neighbor_weights[offset_index].reshape(GX, GY, 1) * gridded
        padded = jnp.pad(weighted, ((1, 1), (1, 1), (0, 0)))
        summed = summed + padded[1 - shift_x : 1 - shift_x + GX, 1 - shift_y : 1 - shift_y + GY]
    return summed.reshape(GX * GY, columns)


def combine_filter(earlier, later):
    trans_early, shift_early, root_early, vec_early, mat_early, flag_early = earlier
    trans_late, shift_late, root_late, vec_late, mat_late, flag_late = later
    eye_mat = jnp.eye(root_early.shape[0], dtype=jnp.float32)
    cross_mat = high_dot(root_early.T, mat_late)
    middle = eye_mat + high_dot(cross_mat, root_early)
    chol_mid = jnp.linalg.cholesky(middle)
    proj_mat = tri_solve(chol_mid, cross_mat)
    wide_mat = tri_solve(chol_mid, root_early.T).T
    moved_mat = trans_early - high_dot(wide_mat, high_dot(proj_mat, trans_early))
    trans_new = high_dot(trans_late, moved_mat)
    carried = shift_early + high_dot(root_early, high_dot(root_early.T, vec_late))
    carried = carried - high_dot(wide_mat, high_dot(proj_mat, carried))
    shift_new = high_dot(trans_late, carried) + shift_late
    spread = high_dot(trans_late, wide_mat)
    both_empty = flag_early * flag_late
    gram_mat = high_dot(spread, spread.T) + high_dot(root_late, root_late.T) + both_empty * eye_mat
    root_new = jnp.linalg.cholesky(gram_mat) * (1.0 - both_empty)
    residual = vec_late - high_dot(mat_late, shift_early)
    residual = residual - high_dot(proj_mat.T, high_dot(wide_mat.T, residual))
    vec_new = high_dot(trans_early.T, residual) + vec_early
    info_mid = mat_late - high_dot(proj_mat.T, proj_mat)
    mat_new = high_dot(trans_early.T, high_dot(info_mid, trans_early)) + mat_early
    return (trans_new, shift_new, root_new, vec_new, mat_new, both_empty)


def smooth_join(lower_elem, higher_elem):
    gain_low, offset_low, cov_low = lower_elem
    gain_high, offset_high, cov_high = higher_elem
    return (
        high_dot(gain_low, gain_high),
        high_dot(gain_low, offset_high) + offset_low,
        high_dot(gain_low, high_dot(cov_high, gain_low.T)) + cov_low,
    )


def log_density(pred_mean, pred_cov, obs_row, mask_row, obs_var):
    mask_val = mask_row.astype(jnp.float32)
    innov_cov = mask_val[:, None] * pred_cov * mask_val[None, :] + jnp.diag(obs_var)
    chol_s = jnp.linalg.cholesky(innov_cov)
    innov = mask_val * (obs_row - pred_mean)
    whitened = tri_solve(chol_s, innov)
    logdet = 2.0 * jnp.sum(jnp.log(jnp.diagonal(chol_s)))
    cell_count = pred_mean.shape[0]
    return -(
        logdet
        - jnp.sum((1.0 - mask_val) * jnp.log(obs_var))
        + jnp.sum(whitened * whitened)
        + jnp.sum(mask_val) * LOG_TWO_PI
    ) / (2.0 * cell_count)


def local(
    observed, obs_mask, prior_mean, prior_var, neighbor_weights, damping, process_var, obs_var
):
    local_steps = observed.shape[0]
    cell_count = observed.shape[1]
    eye_mat = jnp.eye(cell_count, dtype=jnp.float32)
    step_ids = lax.axis_index("tm") * local_steps + jnp.arange(local_steps, dtype=jnp.int32)
    total_steps = local_steps * lax.axis_size("tm")
    dyn_mat = advance(eye_mat, neighbor_weights, damping)
    mask_val = obs_mask.astype(jnp.float32)
    is_first = (step_ids == 0)[:, None]
    post_var = 1.0 / (1.0 / process_var[None, :] + mask_val / obs_var[None, :])
    first_var = 1.0 / (1.0 / prior_var[None, :] + mask_val / obs_var[None, :])
    elem_var = jnp.where(is_first, first_var, post_var)
    shift_elem = elem_var * (
        mask_val * observed / obs_var[None, :]
        + jnp.where(is_first, (prior_mean / prior_var)[None, :], 0.0)
    )
    scale_rows = jnp.where(is_first, 0.0, post_var / process_var[None, :])
    trans_elem = scale_rows[:, :, None] * dyn_mat[None]
    root_elem = jnp.sqrt(elem_var)[:, :, None] * eye_mat[None]
    info_weight = jnp.where(is_first, 0.0, mask_val / (process_var + obs_var)[None, :])
    vec_elem = retreat((info_weight * observed).T, neighbor_weights, damping).T
    mat_elem = jax.vmap(
        lambda weight_row: retreat(weight_row[:, None] * dyn_mat, neighbor_weights, damping)
    )(info_weight)
    flag_elem = jnp.zeros((local_steps,), jnp.float32)
    elements = (trans_elem, shift_elem, root_elem, vec_elem, mat_elem, flag_elem)
    head_elem = jax.tree.map(lambda array_leaf: array_leaf[0], elements)
    tail_elems = jax.tree.map(lambda array_leaf: array_leaf[1:], elements)

    def fold_step(state_in, single):
        joined = combine_filter(state_in, single)
        return (joined, joined)

    aggregate, partial_value = lax.scan(fold_step, head_elem, tail_elems)
    inclusive = jax.tree.map(
        lambda first_leaf, rest_leaf: jnp.concatenate([first_leaf[None], rest_leaf], axis=0),
        head_elem,
        partial_value,
    )
    zero_vec = jnp.zeros((cell_count,), jnp.float32)
    zero_mat = jnp.zeros((cell_count, cell_count), jnp.float32)
    identity_filter = (eye_mat, zero_vec, zero_mat, zero_vec, zero_mat, jnp.float32(1.0))
    prefix = carried_in(aggregate, "tm", combine_filter, identity_filter, False)
    joined_all = jax.vmap(lambda single: combine_filter(prefix, single))(inclusive)
    filt_means = joined_all[1]
    filt_factors = joined_all[2]
    boundary_mean, boundary_factor = from_behind((filt_means[-1], filt_factors[-1]), "tm", 1)
    prev_means = jnp.concatenate([boundary_mean[None], filt_means[:-1]], axis=0)
    prev_factors = jnp.concatenate([boundary_factor[None], filt_factors[:-1]], axis=0)
    pred_means = advance(prev_means.T, neighbor_weights, damping).T
    prev_moved = jax.vmap(lambda factor: advance(factor, neighbor_weights, damping))(prev_factors)
    pred_covs = (
        jax.vmap(lambda moved_one: high_dot(moved_one, moved_one.T))(prev_moved)
        + jnp.diag(process_var)[None]
    )
    pred_means = jnp.where(is_first, prior_mean[None, :], pred_means)
    pred_covs = jnp.where(is_first[:, :, None], jnp.diag(prior_var)[None], pred_covs)
    loglik = jax.vmap(log_density, in_axes=(0, 0, 0, 0, None))(
        pred_means, pred_covs, observed, obs_mask, obs_var
    )
    filt_covs = jax.vmap(lambda factor: high_dot(factor, factor.T))(filt_factors)
    moved_covs = jax.vmap(lambda cov_in: advance(cov_in, neighbor_weights, damping))(filt_covs)
    moved_factors = jax.vmap(lambda factor: advance(factor, neighbor_weights, damping))(
        filt_factors
    )
    next_pred = (
        jax.vmap(lambda moved_one: high_dot(moved_one, moved_one.T))(moved_factors)
        + jnp.diag(process_var)[None]
    )

    def gain_matrix(pred_cov, moved_cov):
        chol_p = jnp.linalg.cholesky(pred_cov)
        return jax.scipy.linalg.cho_solve((chol_p, True), moved_cov).T

    gains = jax.vmap(gain_matrix)(next_pred, moved_covs)
    is_last = (step_ids == total_steps - 1)[:, None, None]
    gains = jnp.where(is_last, 0.0, gains)
    moved_means = advance(filt_means.T, neighbor_weights, damping).T
    offsets = filt_means - jax.vmap(high_dot)(gains, moved_means)
    lower_covs = filt_covs - jax.vmap(high_dot)(gains, moved_covs)
    smooth_elems = (gains, offsets, lower_covs)
    last_elem = jax.tree.map(lambda array_leaf: array_leaf[-1], smooth_elems)
    front_elems = jax.tree.map(lambda array_leaf: array_leaf[:-1], smooth_elems)

    def back_step(state_in, single):
        joined = smooth_join(single, state_in)
        return (joined, joined)

    block_elem, back_partial = lax.scan(back_step, last_elem, front_elems, reverse=True)
    back_inclusive = jax.tree.map(
        lambda rest_leaf, last_leaf: jnp.concatenate([rest_leaf, last_leaf[None]], axis=0),
        back_partial,
        last_elem,
    )
    identity_smooth = (eye_mat, zero_vec, zero_mat)
    suffix = carried_in(
        block_elem,
        "tm",
        lambda higher_elem, lower_elem: smooth_join(lower_elem, higher_elem),
        identity_smooth,
        True,
    )
    smoothed = jax.vmap(lambda single: smooth_join(single, suffix))(back_inclusive)
    smoothed_mean = smoothed[1]
    smoothed_cov = smoothed[2]
    return (smoothed_mean, smoothed_cov, loglik)


def solution(mesh):
    return jax.shard_map(
        local,
        mesh=mesh,
        in_specs=(
            P(("parts", "tm"), None),
            P(("parts", "tm"), None),
            P("parts"),
            P("parts"),
            P(),
            P(),
            P(),
            P(),
        ),
        out_specs=(P(("parts", "tm"), None), P(("parts", "tm"), None, None), P(("parts", "tm"))),
        check_vma=False,
    )
```

profile of v0, /device:TPU:0, one launch (start us, length us, event | category | flops | bytes accessed | tf_op | source)
XLA Modules:
  0.0 1148.4 jit_solution(10118844436278953902)
XLA Ops:
  14.2 11.7 %cholesky.169 = f32[128,128]{1,0:T(8,128)S(1)} custom-call(f32[128,128]{1,0:T(8,128)S(1)} %fusion.220), custom_call_target="Cholesky" | custom-call | tf_op jit(solution)/shard_map/while/body/eval_jaxpr/jit(cholesky)/cholesky | solution.py:83
  41.8 11.7 %cholesky.180 = f32[128,128]{1,0:T(8,128)S(1)} custom-call(f32[128,128]{1,0:T(8,128)S(1)} %fusion.211), custom_call_target="Cholesky" | custom-call | tf_op jit(solution)/shard_map/while/body/eval_jaxpr/jit(cholesky)/cholesky | solution.py:94
  56.8 23.0 %all-gather.8 = f32[16,1,128]{2,1,0:T(1,128)S(1)} all-gather(f32[1,1,128]{2,1,0:T(1,128)S(1)} %bitcast.573), channel_id=3, replica_groups=mesh['parts'=2,'tm'=16] {'tm'}, dimensions={0}, use_global_device_ids=true | all-gather | bytes 8704 | tf_op jit(solution)/shard_map/all_gather | solution.py:18
  81.2 29.9 %all-reduce.22 = f32[16]{0:T(128)S(1)} all-reduce(f32[16]{0:T(128)S(1)} %dynamic-update-slice.4), channel_id=1, replica_groups=mesh['parts'=2,'tm'=16] {'tm'}, use_global_device_ids=true, to_apply=%add.22 | all-reduce | flops 16 | bytes 128
  111.9 17.1 %all-gather.9 = f32[16,1,128]{2,1,0:T(1,128)S(1)} all-gather(f32[1,1,128]{2,1,0:T(1,128)S(1)} %bitcast.568), channel_id=5, replica_groups=mesh['parts'=2,'tm'=16] {'tm'}, dimensions={0}, use_global_device_ids=true | all-gather | bytes 8704 | tf_op jit(solution)/shard_map/all_gather | solution.py:18
  129.7 29.2 %all-gather.21.cloned.1.call-done = f32[2048,128]{1,0:T(8,128)} async-done(((f32[128,128]{1,0:T(8,128)}), f32[2048,128]{1,0:T(8,128)}) %all-gather.21.cloned.1.call-update) | async-done | bytes 1048592 | tf_op jit(solution)/shard_map/all_gather | solution.py:18
  158.9 705.2 %while.23 = (s32[]{:T(128)}, f32[128]{0:T(128)S(1)}, f32[128,128]{1,0:T(8,128)S(1)}, f32[]{:T(128)}, s32[]{:T(128)}, /*index=5*/f32[16,128,128]{2,1,0:T(8,128)},...) while((s32[]{:T(128)}, f32[128]{0:T(128)S(1)}, ...), condition=%wide.region_4.7_spmd.clone, body=%wide.region_3.6_spmd.clone.sunk | while | flops 177669120 | bytes 2764019 | solution.py:31
  160.8 11.7 %cholesky.372 = f32[128,128]{1,0:T(8,128)S(1)} custom-call(f32[128,128]{1,0:T(8,128)S(1)} %fusion.468), custom_call_target="Cholesky" | custom-call | tf_op jit(solution)/shard_map/while/body/eval_jaxpr/jit(cholesky)/cholesky | solution.py:83
  189.4 11.7 %cholesky.373 = f32[128,128]{1,0:T(8,128)S(1)} custom-call(f32[128,128]{1,0:T(8,128)S(1)} %fusion.477), custom_call_target="Cholesky" | custom-call | tf_op jit(solution)/shard_map/while/body/eval_jaxpr/jit(cholesky)/cholesky | solution.py:94
  204.3 11.7 %cholesky.372 = f32[128,128]{1,0:T(8,128)S(1)} custom-call(f32[128,128]{1,0:T(8,128)S(1)} %fusion.468), custom_call_target="Cholesky" | custom-call | tf_op jit(solution)/shard_map/while/body/eval_jaxpr/jit(cholesky)/cholesky | solution.py:83
  232.9 11.7 %cholesky.373 = f32[128,128]{1,0:T(8,128)S(1)} custom-call(f32[128,128]{1,0:T(8,128)S(1)} %fusion.477), custom_call_target="Cholesky" | custom-call | tf_op jit(solution)/shard_map/while/body/eval_jaxpr/jit(cholesky)/cholesky | solution.py:94
  247.8 11.7 %cholesky.372 = f32[128,128]{1,0:T(8,128)S(1)} custom-call(f32[128,128]{1,0:T(8,128)S(1)} %fusion.468), custom_call_target="Cholesky" | custom-call | tf_op jit(solution)/shard_map/while/body/eval_jaxpr/jit(cholesky)/cholesky | solution.py:83
  276.4 11.7 %cholesky.373 = f32[128,128]{1,0:T(8,128)S(1)} custom-call(f32[128,128]{1,0:T(8,128)S(1)} %fusion.477), custom_call_target="Cholesky" | custom-call | tf_op jit(solution)/shard_map/while/body/eval_jaxpr/jit(cholesky)/cholesky | solution.py:94
  291.3 11.7 %cholesky.372 = f32[128,128]{1,0:T(8,128)S(1)} custom-call(f32[128,128]{1,0:T(8,128)S(1)} %fusion.468), custom_call_target="Cholesky" | custom-call | tf_op jit(solution)/shard_map/while/body/eval_jaxpr/jit(cholesky)/cholesky | solution.py:83
  363.4 11.7 %cholesky.373 = f32[128,128]{1,0:T(8,128)S(1)} custom-call(f32[128,128]{1,0:T(8,128)S(1)} %fusion.477), custom_call_target="Cholesky" | custom-call | tf_op jit(solution)/shard_map/while/body/eval_jaxpr/jit(cholesky)/cholesky | solution.py:94
  378.3 11.7 %cholesky.372 = f32[128,128]{1,0:T(8,128)S(1)} custom-call(f32[128,128]{1,0:T(8,128)S(1)} %fusion.468), custom_call_target="Cholesky" | custom-call | tf_op jit(solution)/shard_map/while/body/eval_jaxpr/jit(cholesky)/cholesky | solution.py:83
  406.9 11.7 %cholesky.373 = f32[128,128]{1,0:T(8,128)S(1)} custom-call(f32[128,128]{1,0:T(8,128)S(1)} %fusion.477), custom_call_target="Cholesky" | custom-call | tf_op jit(solution)/shard_map/while/body/eval_jaxpr/jit(cholesky)/cholesky | solution.py:94
  421.8 11.7 %cholesky.372 = f32[128,128]{1,0:T(8,128)S(1)} custom-call(f32[128,128]{1,0:T(8,128)S(1)} %fusion.468), custom_call_target="Cholesky" | custom-call | tf_op jit(solution)/shard_map/while/body/eval_jaxpr/jit(cholesky)/cholesky | solution.py:83
  624.3 11.7 %cholesky.373 = f32[128,128]{1,0:T(8,128)S(1)} custom-call(f32[128,128]{1,0:T(8,128)S(1)} %fusion.477), custom_call_target="Cholesky" | custom-call | tf_op jit(solution)/shard_map/while/body/eval_jaxpr/jit(cholesky)/cholesky | solution.py:94
  667.8 11.7 %cholesky.373 = f32[128,128]{1,0:T(8,128)S(1)} custom-call(f32[128,128]{1,0:T(8,128)S(1)} %fusion.477), custom_call_target="Cholesky" | custom-call | tf_op jit(solution)/shard_map/while/body/eval_jaxpr/jit(cholesky)/cholesky | solution.py:94
  682.7 11.7 %cholesky.372 = f32[128,128]{1,0:T(8,128)S(1)} custom-call(f32[128,128]{1,0:T(8,128)S(1)} %fusion.468), custom_call_target="Cholesky" | custom-call | tf_op jit(solution)/shard_map/while/body/eval_jaxpr/jit(cholesky)/cholesky | solution.py:83
  726.2 11.7 %cholesky.372 = f32[128,128]{1,0:T(8,128)S(1)} custom-call(f32[128,128]{1,0:T(8,128)S(1)} %fusion.468), custom_call_target="Cholesky" | custom-call | tf_op jit(solution)/shard_map/while/body/eval_jaxpr/jit(cholesky)/cholesky | solution.py:83
  864.9 23.5 %custom-call.39 = f32[2,128,128]{2,1,0:T(8,128)S(1)} custom-call(f32[2,128,128]{2,1,0:T(8,128)S(1)} %fusion.173), custom_call_target="Cholesky" | custom-call | tf_op jit(solution)/shard_map/vmap(jit(cholesky))/cholesky | solution.py:83
  888.6 19.7 %custom-call.40 = f32[2,1,128,128]{2,3,1,0:T(8,128)S(1)} custom-call(f32[2,1,128,128]{3,2,1,0:T(8,128)S(1)} %select_bitcast_fusion.1), custom_call_target="InvertDiagBlocksLowerTriangular" | custom-call | tf_op jit(solution)/shard_map/vmap(jit(_solve_triangular))/triangular_solve/custom-call.3 | solution.py:45
  910.1 23.5 %custom-call.41 = f32[2,128,128]{2,1,0:T(8,128)S(1)} custom-call(f32[2,128,128]{2,1,0:T(8,128)S(1)} %fusion.185), custom_call_target="Cholesky" | custom-call | tf_op jit(solution)/shard_map/vmap(jit(cholesky))/cholesky | solution.py:94
  938.1 23.7 %custom-call.42 = f32[2,128,128]{2,1,0:T(8,128)S(1)} custom-call(f32[2,128,128]{2,1,0:T(8,128)S(1)} %fusion.184), custom_call_target="Cholesky" | custom-call | tf_op jit(solution)/shard_map/vmap(jit(cholesky))/cholesky | solution.py:202
  962.6 23.5 %custom-call.45 = f32[2,128,128]{2,1,0:T(8,128)S(1)} custom-call(f32[2,128,128]{2,1,0:T(8,128)S(1)} %fusion.176), custom_call_target="Cholesky" | custom-call | tf_op jit(solution)/shard_map/vmap(jit(cholesky))/cholesky | solution.py:116
  986.5 19.7 %custom-call.43 = f32[2,1,128,128]{2,3,1,0:T(8,128)S(1)} custom-call(f32[2,1,128,128]{3,2,1,0:T(8,128)S(1)} %get-tuple-element.585), custom_call_target="InvertDiagBlocksLowerTriangular" | custom-call | tf_op jit(solution)/shard_map/vmap(jit(_cho_solve))/triangular_solve/custom-call.3 | solution.py:203
  1013.9 19.7 %custom-call.20 = f32[2,1,128,128]{2,3,1,0:T(8,128)S(1)} custom-call(f32[2,1,128,128]{3,2,1,0:T(8,128)S(1)} %get-tuple-element.567), custom_call_target="InvertDiagBlocksLowerTriangular" | custom-call | tf_op jit(solution)/shard_map/vmap(jit(_solve_triangular))/triangular_solve | solution.py:45
  1040.2 20.1 %all-gather.10 = f32[16,1,128]{2,1,0:T(1,128)S(1)} all-gather(f32[1,1,128]{2,1,0:T(1,128)S(1)} %bitcast.575), channel_id=8, replica_groups=mesh['parts'=2,'tm'=16] {'tm'}, dimensions={0}, use_global_device_ids=true | all-gather | bytes 8704 | tf_op jit(solution)/shard_map/all_gather | solution.py:18
  1061.2 24.3 %all-gather.25.cloned.1.call-done = f32[2048,128]{1,0:T(8,128)} async-done(((f32[128,128]{1,0:T(8,128)}), f32[2048,128]{1,0:T(8,128)}) %all-gather.25.cloned.1.call-update) | async-done | bytes 1048592 | tf_op jit(solution)/shard_map/all_gather | solution.py:18
  1085.4 54.0 %while.24 = (s32[]{:T(128)}, f32[128]{0:T(128)S(1)}, f32[128,128]{1,0:T(8,128)S(1)}, s32[]{:T(128)}, f32[16,128,128]{2,1,0:T(8,128)}, /*index=5*/f32[16,128]{1,0...) while((s32[]{:T(128)}, f32[128]{0:T(128)S(1)}, ...), condition=%wide.region_8.13_spmd.clone, body=%wide.region_7.12_spmd.clone.sunk | while | flops 50594312 | bytes 597690 | solution.py:31
  (660 shorter events, 617.1 us)
Async XLA Ops:
  7.2 72.7 %copy-start.10 = (u32[32]{0:T(128)S(1)}, u32[32]{0:T(128)}, u32[]{:S(2)}) copy-start(u32[32]{0:T(128)} %constant.303) | copy-start | bytes 388
  7.2 122.4 %copy-start.8 = (f32[128]{0:T(128)S(1)}, f32[128]{0:T(128)}, u32[]{:S(2)}) copy-start(f32[128]{0:T(128)} %param.21) | copy-start | bytes 1540
  7.2 121.8 %copy-start.5 = (f32[128]{0:T(128)S(1)}, f32[128]{0:T(128)}, u32[]{:S(2)}) copy-start(f32[128]{0:T(128)} %param.24) | copy-start | bytes 1540
  7.2 122.4 %copy-start.6 = (f32[128]{0:T(128)S(1)}, f32[128]{0:T(128)}, u32[]{:S(2)}) copy-start(f32[128]{0:T(128)} %param.25) | copy-start | bytes 1540
  7.2 48.3 %copy-start.4 = (s32[2,128]{1,0:T(2,128)S(1)}, s32[2,128]{1,0:T(2,128)}, u32[]{:S(2)}) copy-start(s32[2,128]{1,0:T(2,128)} %param.19) | copy-start | bytes 3076
  7.2 122.4 %all-gather.17.cloned.1.call-start = ((), (), s32[]{:S(2)}) async-start(), calls=%async_computation | async-start | bytes 1114112 | tf_op jit(solution)/shard_map/all_gather | solution.py:18
  39.1 90.6 %all-gather.19.cloned.1.call-start = ((), (), s32[]{:S(2)}) async-start(), calls=%async_computation.1 | async-start | bytes 1114112 | tf_op jit(solution)/shard_map/all_gather | solution.py:18
  40.6 118.3 %all-gather.21.cloned.1.call-start = ((), (), s32[]{:S(2)}) async-start(), calls=%async_computation.2 | async-start | bytes 1114112 | tf_op jit(solution)/shard_map/all_gather | solution.py:18
  41.8 822.2 %copy-start.2 = (f32[128,128]{1,0:T(8,128)S(1)}, f32[128,128]{1,0:T(8,128)}, u32[]{:S(2)}) copy-start(f32[128,128]{1,0:T(8,128)} %convolution_add_fusion.10) | copy-start | bytes 196612
  55.5 1005.7 %all-gather.23.cloned.1.call-start = ((), (), s32[]{:S(2)}) async-start(), calls=%async_computation.3 | async-start | bytes 1114112 | tf_op jit(solution)/shard_map/all_gather | solution.py:18
  158.9 749.9 %copy-start.1 = (f32[128,128]{1,0:T(8,128)S(1)}, f32[128,128]{1,0:T(8,128)}, u32[]{:S(2)}) copy-start(f32[128,128]{1,0:T(8,128)} %fusion.255) | copy-start | bytes 196612
  864.0 149.4 %copy-start.7 = (f32[2,128]{1,0:T(2,128)S(1)}, f32[2,128]{1,0:T(2,128)}, u32[]{:S(2)}) copy-start(f32[2,128]{1,0:T(2,128)} %param.18) | copy-start | bytes 3076
  864.0 149.4 %copy-start.9 = (f32[128]{0:T(128)S(1)}, f32[128]{0:T(128)}, u32[]{:S(2)}) copy-start(f32[128]{0:T(128)} %param.20) | copy-start | bytes 1540
  934.9 26.8 %collective-permute-start = (f32[128,128]{1,0:T(8,128)S(1)}, f32[128,128]{1,0:T(8,128)S(1)}, u32[]{:S(2)}, u32[]{:S(2)}) collective-permute-start(f32[128,128]{1,0:T(8,128)S(1)} %get-tuple-element.573), channel_id=1, source_target_pairs={{0,1},{1,2},{2,3},{3,4},{4,5},{5,6},{6,7},{7,8},{8,9},{9,10},{10,1... | collective-permute-start | bytes 196616 | tf_op jit(solution)/shard_map/ppermute | solution.py:37
  1007.8 131.6 %copy-start = (f32[128,128]{1,0:T(8,128)S(1)}, f32[128,128]{1,0:T(8,128)}, u32[]{:S(2)}) copy-start(f32[128,128]{1,0:T(8,128)} %fusion.207) | copy-start | bytes 196612
  1007.8 77.6 %all-gather.25.cloned.1.call-start = ((), (), s32[]{:S(2)}) async-start(), calls=%async_computation.4 | async-start | bytes 1114112 | tf_op jit(solution)/shard_map/all_gather | solution.py:18
  1009.0 4.0 collective-permute-start.1
  1012.9 127.6 %copy-start.3 = (f32[128,128]{1,0:T(8,128)S(1)}, f32[128,128]{1,0:T(8,128)}, u32[]{:S(2)}) copy-start(f32[128,128]{1,0:T(8,128)} %convolution_add_fusion.8) | copy-start | bytes 196612
Sparse Core Ops, SparseCore 0:
  39.2 40.9 all-gather.16
  82.9 36.7 all-gather.18
  121.9 36.8 all-gather.20
  1007.9 38.5 all-gather.22
  1048.5 36.8 all-gather.24
where the time goes:
time: 1160 us; the launch traced here: 1150 us
  other arithmetic  768 us (66%)
  matrix products  173 us (15%)
  blocking collectives  90 us (8%)
  waiting for transfers between devices  53.6 us (5%)
  local copies, waits for them, and re-layouts  22.9 us (2%)
  loops' own time  20.7 us (2%)
  between operations  15 us (1%)
    another operation x54, other arithmetic, combine_filter(): root_new = jnp.linalg.cholesky(gram_mat) * (1.0 - both_empty)  234 us
    another operation x54, other arithmetic, combine_filter(): chol_mid = jnp.linalg.cholesky(middle)  234 us
    another operation x38, other arithmetic, tri_solve(): return jax.scipy.linalg.solve_triangular(lower_mat, rhs, lower=True)  216 us
    dot_general x250, matrix products, high_dot(): jnp.dot(left, right, precision=lax.Precision.HIGHEST, preferred_element_t...  161 us
    all_gather x3, blocking collectives, carried_in(): everything = jax.tree.map(lambda part: lax.all_gather(part, axis), array)  60.1 us
    all_gather x5, waiting for transfers between devices, carried_in(): everything = jax.tree.map(lambda part: lax.all_gather(part, axis), array)  53.5 us
    unnamed x1, blocking collectives  29.9 us
    another operation x3, other arithmetic, gain_matrix(): chol_p = jnp.linalg.cholesky(pred_cov)  23.8 us
  transfers between devices with their start and end apart: 7, of which 2 were waited for; matrix products, arithmetic and copies ran while one was open for 7% of the time, Pallas kernels for 0%

commit v1 on v0

v1 whole, which is shorter than its diff:
```python
import functools
import math

import jax
import jax.numpy as jnp
from jax import lax
from jax.experimental import pallas as pl
from jax.experimental.pallas import tpu as pltpu
from jax.sharding import PartitionSpec as P

GX = 16
GY = 8
OFFSETS = ((-1, -1), (-1, 0), (-1, 1), (0, -1), (0, 1), (1, -1), (1, 0), (1, 1))
LOG_TWO_PI = math.log(2.0 * math.pi)

WINDOW = 4
SLOTS = 48
FAR = 1 << 29

NN = (((1,), (0,)), ((), ()))
NT = (((1,), (1,)), ((), ()))
TN = (((0,), (0,)), ((), ()))
BF = jnp.bfloat16
F32 = jnp.float32


def halves(x):
    high = x.astype(BF)
    return high, (x - high.astype(F32)).astype(BF)


def as_left(x, axis):
    high, low = halves(x)
    return jnp.concatenate([high, high, low], axis=axis)


def as_right(x, axis):
    high, low = halves(x)
    return jnp.concatenate([high, low, high], axis=axis)


def raw(left, right, dims):
    return lax.dot_general(left, right, dims, preferred_element_type=F32)


def dot(left, right, dims=NN):
    (left_axis,), (right_axis,) = dims[0]
    return raw(as_left(left, left_axis), as_right(right, right_axis), dims)


def exact_dot(ones_left, right, dims=NN):
    (left_axis,), (right_axis,) = dims[0]
    high, low = halves(right)
    left = ones_left.astype(BF)
    return raw(
        jnp.concatenate([left, left], axis=left_axis),
        jnp.concatenate([high, low], axis=right_axis),
        dims,
    )


def iota(shape, axis):
    return lax.broadcasted_iota(jnp.int32, shape, axis)


def transition(nw, damping):
    size = GX * GY
    source, cell = iota((size, size), 0), iota((size, size), 1)
    row, column = cell // GY, cell % GY
    source_row, source_column = source // GY, source % GY
    centre = 1.0 - jnp.sum(nw, axis=0, keepdims=True) - damping
    flipped = jnp.where(source == cell, centre, 0.0)
    for index, (dx, dy) in enumerate(OFFSETS):
        hit = (source_row == row + dx) & (source_column == column + dy)
        flipped = flipped + jnp.where(hit, nw[index : index + 1, :], 0.0)
    return jnp.transpose(flipped)


def eliminate(square, sides):
    tiles = SLOTS // 8
    rows = iota((8, 128), 0)
    columns = {}
    for k in range(SLOTS - 1):
        for tile in range(k // 8, tiles):
            block = square[8 * tile : 8 * tile + 8, k : k + 1]
            columns[k, tile] = jnp.broadcast_to(block, (8, 128))
    parts = [[side[8 * t : 8 * t + 8, :] for t in range(tiles)] for side in sides]
    pivots = [jnp.ones((8, 128), F32) for _ in range(tiles)]
    quad = jnp.zeros((8, 128), F32)

    def spread(block, row):
        return jnp.broadcast_to(block[row : row + 1, :], (8, 128))

    for j in range(SLOTS - 1):
        home, row = divmod(j, 8)
        pivot = spread(columns[j, home], row)
        pivots[home] = jnp.where(rows == row, pivot, pivots[home])
        inverse = 1.0 / pivot
        weights = {}
        for tile in range(home, tiles):
            scaled = columns[j, tile] * inverse
            if tile == home:
                scaled = jnp.where(rows > row, scaled, 0.0)
            weights[tile] = scaled
        quad = quad + weights[tiles - 1] * columns[j, tiles - 1]
        for k in range(j + 1, SLOTS - 1):
            across = spread(columns[k, k // 8], row) if k // 8 == home else None
            if across is None:
                across = spread(columns[j, k // 8], k % 8)
            for tile in range(k // 8, tiles):
                columns[k, tile] = columns[k, tile] - weights[tile] * across
        for part in parts:
            across = spread(part[home], row)
            for tile in range(home, tiles):
                part[tile] = part[tile] - weights[tile] * across
    pivots = jnp.concatenate(pivots, axis=0)
    sides = [jnp.concatenate(part, axis=0) for part in parts]
    return sides, pivots, quad[7:8, :]


def chain_kernel(
    own,
    position_ref,
    gathered_ref,
    mean_ref,
    var_ref,
    nw_ref,
    damping_ref,
    process_ref,
    noise_ref,
    smooth_mean_ref,
    smooth_cov_ref,
    loglik_ref,
    mask_s,
    obs_s,
    rank_s,
    off_v,
    off_s,
    power_s,
    left_s,
    right_s,
    big_s,
    psi_s,
    added_s,
    cov_s,
    trans_s,
    info_s,
    mean_s,
    pull_s,
    kept_cov,
    kept_mean,
    kept_trans,
    kept_info,
    kept_pull,
    kept_lik,
    sem,
):
    size = GX * GY
    steps = gathered_ref.shape[0]
    padded = mask_s.shape[0]
    position = position_ref[0]
    base = position * own
    nw, damping = nw_ref[...], damping_ref[...]
    process, noise = process_ref[...], noise_ref[...]

    mask_s[...] = jnp.zeros_like(mask_s)
    obs_s[...] = jnp.zeros_like(obs_s)
    for block in range(steps // own):
        held = (position_ref[1] ^ block) * own
        for row in range(own):
            at = block * own + row
            line = gathered_ref[pl.ds(held + row, 1), :]
            obs_s[at : at + 1, :] = line[:, :size]
            mask_s[at : at + 1, :] = line[:, size:]
    mask = mask_s[...]
    mask_b = mask.astype(BF)
    before = (iota((padded, padded), 0) < iota((padded, padded), 1)).astype(BF)
    after = (iota((padded, padded), 0) > iota((padded, padded), 1)).astype(BF)
    counts_row = raw(jnp.ones((8, size), BF), mask_b, NT)
    off_v[...] = raw(counts_row.astype(BF), before, NN).astype(jnp.int32)
    copy = pltpu.make_async_copy(off_v, off_s, sem)
    copy.start()
    counts = raw(mask_b, jnp.ones((size, size), BF), NN)
    within = (iota((size, size), 0) < iota((size, size), 1)).astype(BF)
    rank = raw(mask_b, within, NN) + raw(after, counts.astype(BF), NN)
    rank_s[...] = jnp.where(mask > 0.0, rank.astype(jnp.int32), FAR)

    eye = (iota((size, size), 0) == iota((size, size), 1)).astype(F32)
    power_s[0] = eye
    power_s[1] = transition(nw, damping)
    for e in range(2, WINDOW + 1):
        power_s[e] = dot(power_s[(e + 1) // 2], power_s[e // 2])
    psi_s[...] = jnp.zeros_like(psi_s)
    big_s[...] = jnp.zeros_like(big_s)
    added_s[0] = jnp.zeros((size, size), F32)
    wide = (WINDOW - 1) * size
    for e in range(WINDOW + 1):
        left_s[e] = as_left(power_s[e], 1)
        right_s[e] = as_right(power_s[e], 1)
        if e >= 1:
            moved = power_s[e - 1]
            added_s[e] = added_s[e - 1] + dot(moved * process, moved, NT)
        for l in range(1, min(e, WINDOW - 1) + 1):
            high, low = halves(power_s[e - l])
            for piece, held in enumerate((high, low, high)):
                psi_s[e, :, piece * wide + (l - 1) * size : piece * wide + l * size] = held
    for i in range(1, WINDOW):
        for l in range(0, i):
            high, low = halves(power_s[i - l])
            for piece, held in enumerate((high, low)):
                start = piece * wide + (i - 1) * size
                big_s[start : start + size, l * size : (l + 1) * size] = held

    cov_s[...] = eye * var_ref[...]
    mean_s[...] = mean_ref[...]
    trans_s[...] = jnp.zeros_like(trans_s)
    info_s[...] = jnp.zeros_like(info_s)
    pull_s[...] = jnp.zeros_like(pull_s)
    kept_lik[...] = jnp.zeros_like(kept_lik)
    copy.wait()
    last_row = iota((SLOTS, 1), 0) == SLOTS - 1

    def body(state):
        step, first = state
        inside = (step >= base) & (step < base + own)
        cut = jnp.where(step < base, base, jnp.where(inside, step + 1, steps))
        end = jnp.minimum(step + WINDOW, cut)
        taken = jnp.minimum(off_s[0, end] - first, SLOTS - 1)
        ahead = jnp.int32(0)
        for i in range(1, WINDOW + 1):
            done = (step + i <= end) & (off_s[0, step + i] <= first + taken)
            ahead = ahead + done.astype(jnp.int32)
        mine = jnp.clip(step - base, 0, own - 1)

        @pl.when(inside & (first == off_s[0, step]))
        def _():
            kept_cov[mine] = cov_s[...]
            kept_mean[mine] = mean_s[...]
            kept_trans[mine] = trans_s[...]
            kept_info[mine] = info_s[...]
            kept_pull[mine] = pull_s[...]
            trans_s[...] = eye
            info_s[...] = jnp.zeros_like(info_s)
            pull_s[...] = jnp.zeros_like(pull_s)

        slot = iota((SLOTS, size), 0)
        picks = []
        for i in range(WINDOW):
            where = rank_s[pl.ds(step + i, 1), :] - first
            picks.append(jnp.where((slot == where) & (slot < taken), 1.0, 0.0))
        tail = jnp.concatenate(picks[1:], axis=1).astype(BF)
        spread_out = raw(jnp.concatenate([tail, tail], axis=1), big_s[...], NN)
        watch = picks[0] + spread_out[:, :size]
        shocks = jnp.concatenate(
            [
                picks[l] + (spread_out[:, l * size : (l + 1) * size] if l < WINDOW - 1 else 0.0)
                for l in range(1, WINDOW)
            ],
            axis=1,
        )
        scaled = shocks * jnp.concatenate([process] * (WINDOW - 1), axis=1)
        fixed = raw(
            as_left(scaled, 1),
            jnp.concatenate([as_right(shocks, 1), psi_s[ahead]], axis=0),
            NT,
        )
        readings = jnp.concatenate(
            [
                picks[i] * noise + jnp.where(last_row, -obs_s[pl.ds(step + i, 1), :], 0.0)
                for i in range(WINDOW)
            ],
            axis=1,
        )
        every = jnp.concatenate(picks, axis=1).astype(BF)
        high, low = halves(readings)
        lowest = (readings - high.astype(F32) - low.astype(F32)).astype(BF)
        own_noise = raw(
            jnp.concatenate([high, low, lowest], axis=1),
            jnp.concatenate([every, every, every], axis=1),
            NT,
        )
        diagonal = (iota((SLOTS, SLOTS), 0) == iota((SLOTS, SLOTS), 1)) & (
            iota((SLOTS, SLOTS), 0) >= taken
        )
        own_noise = own_noise + diagonal.astype(F32)

        cov, trans = cov_s[...], trans_s[...]
        cov_right, trans_right = as_right(cov, 0), as_right(trans, 0)
        seen = raw(as_left(watch, 1), jnp.concatenate([cov_right, trans_right], axis=1), NN)
        seen_cov = jnp.where(last_row, mean_s[...], seen[:, :size])
        seen_trans = jnp.where(last_row, pull_s[...], seen[:, size:])
        joint = fixed + raw(
            as_left(seen_cov, 1),
            jnp.concatenate([as_right(watch, 1), right_s[ahead]], axis=0),
            NT,
        )
        moved = raw(left_s[ahead], jnp.concatenate([cov_right, trans_right], axis=1), NN)
        moved_cov = raw(as_left(moved[:, :size], 1), right_s[ahead], NT) + added_s[ahead]
        square = joint[:, :SLOTS] + own_noise
        (to_state, to_trans), pivots, quad = eliminate(square, (joint[:, SLOTS:], seen_trans))
        mean_s[...] = to_state[SLOTS - 1 :, :]
        pull_s[...] = to_trans[SLOTS - 1 :, :]
        scale = jnp.where(last_row, 0.0, lax.rsqrt(pivots))
        factors = jnp.concatenate([to_state * scale, to_trans * scale], axis=1)
        outer = raw(as_left(factors, 0), as_right(factors, 0), TN)
        cov_s[...] = moved_cov - outer[:size, :size]
        trans_s[...] = moved[:, size:] - outer[:size, size:]
        info_s[...] = info_s[...] + outer[size:, size:]

        @pl.when(inside)
        def _():
            log_det = jnp.sum(jnp.log(pivots), axis=0, keepdims=True)
            count = taken.astype(F32) * LOG_TWO_PI
            kept_lik[mine] = kept_lik[mine] + (log_det + quad + count)

        return step + ahead, first + taken

    lax.while_loop(lambda state: state[0] < steps, body, (jnp.int32(0), jnp.int32(0)))

    info, pull = info_s[...], pull_s[...]
    for j in range(own - 1, -1, -1):
        cov = kept_cov[j]
        smooth_cov_ref[j] = cov - dot(dot(cov, info), cov)
        smooth_mean_ref[j : j + 1, :] = kept_mean[j] + dot(pull, cov)
        loglik_ref[j : j + 1, :] = kept_lik[j] * (-1.0 / (2.0 * size))
        if j > 0:
            trans = kept_trans[j]
            info = kept_info[j] + dot(dot(trans, info, TN), trans)
            pull = kept_pull[j] + dot(pull, trans)


def chain(position, gathered, prior_mean, prior_var, nw, damping, process_var, obs_var, own):
    steps, size = gathered.shape[0], gathered.shape[1] // 2
    padded = -(-(steps + WINDOW + 1) // 128) * 128
    wide = (WINDOW - 1) * size
    vmem = pl.BlockSpec(memory_space=pltpu.VMEM)
    square = (size, size)
    return pl.pallas_call(
        functools.partial(chain_kernel, own),
        out_shape=(
            jax.ShapeDtypeStruct((own, size), F32),
            jax.ShapeDtypeStruct((own, size, size), F32),
            jax.ShapeDtypeStruct((own, size), F32),
        ),
        in_specs=[pl.BlockSpec(memory_space=pltpu.SMEM)] + [vmem] * 7,
        out_specs=(vmem, vmem, vmem),
        scratch_shapes=[
            pltpu.VMEM((padded, size), F32),
            pltpu.VMEM((padded, size), F32),
            pltpu.VMEM((padded, size), jnp.int32),
            pltpu.VMEM((8, padded), jnp.int32),
            pltpu.SMEM((8, padded), jnp.int32),
            pltpu.VMEM((WINDOW + 1,) + square, F32),
            pltpu.VMEM((WINDOW + 1, size, 3 * size), BF),
            pltpu.VMEM((WINDOW + 1, size, 3 * size), BF),
            pltpu.VMEM((2 * wide, wide), BF),
            pltpu.VMEM((WINDOW + 1, size, 3 * wide), BF),
            pltpu.VMEM((WINDOW + 1,) + square, F32),
            pltpu.VMEM(square, F32),
            pltpu.VMEM(square, F32),
            pltpu.VMEM(square, F32),
            pltpu.VMEM((1, size), F32),
            pltpu.VMEM((1, size), F32),
            pltpu.VMEM((own,) + square, F32),
            pltpu.VMEM((own, 1, size), F32),
            pltpu.VMEM((own,) + square, F32),
            pltpu.VMEM((own,) + square, F32),
            pltpu.VMEM((own, 1, size), F32),
            pltpu.VMEM((own, 1, size), F32),
            pltpu.SemaphoreType.DMA(()),
        ],
        compiler_params=pltpu.CompilerParams(vmem_limit_bytes=48 * 1024 * 1024),
    )(position, gathered, prior_mean, prior_var, nw, damping, process_var, obs_var)


def gather_all(block, axis):
    size = lax.axis_size(axis)
    held, reach = block, 1
    if size & (size - 1):
        return lax.all_gather(block, axis, tiled=True), jnp.int32(0)
    while reach < size:
        pairs = [(i, i ^ reach) for i in range(size)]
        held = jnp.concatenate([held, lax.ppermute(held, axis, pairs)], axis=0)
        reach *= 2
    return held, lax.axis_index(axis).astype(jnp.int32)


def local(
    observed, obs_mask, prior_mean, prior_var, neighbor_weights, damping, process_var, obs_var
):
    own = observed.shape[0]
    block = jnp.concatenate([observed, obs_mask.astype(F32)], axis=1)
    gathered, flip = gather_all(block, "tm")
    position = jnp.stack([lax.axis_index("tm").astype(jnp.int32), flip])
    smooth_mean, smooth_cov, loglik = chain(
        position,
        gathered,
        prior_mean[None],
        prior_var[None],
        neighbor_weights,
        damping[None],
        process_var[None],
        obs_var[None],
        own,
    )
    return smooth_mean, smooth_cov, loglik[:, 0]


def solution(mesh):
    return jax.shard_map(
        local,
        mesh=mesh,
        in_specs=(
            P(("parts", "tm"), None),
            P(("parts", "tm"), None),
            P("parts"),
            P("parts"),
            P(),
            P(),
            P(),
            P(),
        ),
        out_specs=(P(("parts", "tm"), None), P(("parts", "tm"), None, None), P(("parts", "tm"))),
        check_vma=False,
    )
```

time: 1160 us -> 45.5 us (0.04)
  other arithmetic: 768 us -> 0.79 us
  matrix products: 173 us -> 0 us
  blocking collectives: 90 us -> 0 us
  waiting for transfers between devices: 53.6 us -> 5.68 us
  Pallas kernels: 0 us -> 28.1 us
  local copies, waits for them, and re-layouts: 22.9 us -> 1.34 us
  loops' own time: 20.7 us -> 0 us
  between operations: 15 us -> 0.7 us
    another operation x154 -> x1, other arithmetic: 751 us -> 0.07 us  [local(): position = jnp.stack([lax.axis_index('tm').astype(jnp.int32), flip])]
    dot_general x250 -> x0, matrix products: 161 us -> none  [high_dot(): jnp.dot(left, right, precision=lax.Precision.HIGHEST, preferred_element_t...]
    all_gather x3 -> x0, blocking collectives: 60.1 us -> none  [carried_in(): everything = jax.tree.map(lambda part: lax.all_gather(part, axis), array)]
    all_gather x5 -> x0, waiting for transfers between devices: 53.5 us -> none  [carried_in(): everything = jax.tree.map(lambda part: lax.all_gather(part, axis), array)]
    unnamed x1 -> x0, blocking collectives: 29.9 us -> none
    pallas_call x0 -> x1, Pallas kernels: none -> 28.1 us  [chain(): pl.pallas_call(functools.partial(chain_kernel, own), out_shape=(jax.Shape...]
    another operation x2 -> x0, loops' own time: 20.7 us -> none  [carried_in(): return lax.fori_loop(0, size, lap, start)]
    another operation x39 -> x0, matrix products: 12.2 us -> none  [the longest x37 11.4 us: tri_solve(): return jax.scipy.linalg.solve_triangular(lower_mat, rhs, lower=True)]
  transfers between devices with their start and end apart: 7 -> 4, of which waited for: 2 -> 4; matrix products, arithmetic and copies ran while one was open for 7% -> 0% of each run, Pallas kernels for 0% -> 0%
where the time goes in v1:
time: 45.5 us; the launch traced here: 45.3 us
  Pallas kernels  28.1 us (62%)
  starting transfers between devices  8.66 us (19%)
  waiting for transfers between devices  5.68 us (12%)
  local copies, waits for them, and re-layouts  1.34 us (3%)
  other arithmetic  0.79 us (2%)
  between operations  0.7 us (2%)
    pallas_call x1, Pallas kernels, chain(): pl.pallas_call(functools.partial(chain_kernel, own), out_shape=(jax.Shape...  28.1 us
    ppermute x4, starting transfers between devices, gather_all(): held = jnp.concatenate([held, lax.ppermute(held, axis, pairs)], axis=0)  8.66 us
    ppermute x4, waiting for transfers between devices, gather_all(): held = jnp.concatenate([held, lax.ppermute(held, axis, pairs)], axis=0)  5.68 us
  transfers between devices with their start and end apart: 4, of which 4 were waited for; matrix products, arithmetic and copies ran while one was open for 0% of the time, Pallas kernels for 0%

profile of v1, /device:TPU:0, one launch (start us, length us, event | category | flops | bytes accessed | tf_op | source)
XLA Modules:
  0.0 45.3 jit_solution(1754923379416073026)
XLA Ops:
  0.6 0.0 copy-start.6
  0.6 0.7 %convert_element_type.3 = f32[2,128]{1,0:T(2,128)S(1)} convert(s32[2,128]{1,0:T(2,128)} %param.9) | non-fusion elementwise | flops 256 | bytes 2048 | tf_op jit(solution)/shard_map/convert_element_type | solution.py:392
  1.3 0.0 copy-done.6
  1.3 0.5 %collective-permute-start = (f32[2,256]{1,0:T(2,128)S(1)}, f32[2,256]{1,0:T(2,128)S(1)}, u32[]{:S(2)}, u32[]{:S(2)}) collective-permute-start(f32[2,256]{1,0:T(2,128)S(1)} %pad_maximum_fusion.3), channel_id=1, source_target_pairs={{0,1},{1,0},{2,3},{3,2},{4,5},{5,4},{6,7},{7,6},{8,9},{9,8},{10,11... | collective-permute-start | bytes 6152 | tf_op jit(solution)/shard_map/ppermute | solution.py:383
  1.8 0.8 %collective-permute-done = f32[2,256]{1,0:T(2,128)S(1)} collective-permute-done((f32[2,256]{1,0:T(2,128)S(1)}, f32[2,256]{1,0:T(2,128)S(1)}, u32[]{:S(2)}, u32[]{:S(2)}) %collective-permute-start) | collective-permute-done | bytes 2080 | tf_op jit(solution)/shard_map/ppermute | solution.py:383
  2.7 2.9 %collective-permute-start.1 = (f32[4,256]{1,0:T(4,128)S(1)}, f32[4,256]{1,0:T(4,128)S(1)}, u32[]{:S(2)}, u32[]{:S(2)}) collective-permute-start(f32[4,256]{1,0:T(4,128)S(1)} %pad_maximum_fusion.2), channel_id=1, source_target_pairs={{0,2},{1,3},{2,0},{3,1},{4,6},{5,7},{6,4},{7,5},{8,10},{9,11},{10,... | collective-permute-start | bytes 12296 | tf_op jit(solution)/shard_map/ppermute | solution.py:383
  5.6 1.6 %collective-permute-done.1 = f32[4,256]{1,0:T(4,128)S(1)} collective-permute-done((f32[4,256]{1,0:T(4,128)S(1)}, f32[4,256]{1,0:T(4,128)S(1)}, u32[]{:S(2)}, u32[]{:S(2)}) %collective-permute-start.1) | collective-permute-done | bytes 4128 | tf_op jit(solution)/shard_map/ppermute | solution.py:383
  7.2 2.1 %collective-permute-start.2 = (f32[8,256]{1,0:T(8,128)S(1)}, f32[8,256]{1,0:T(8,128)S(1)}, u32[]{:S(2)}, u32[]{:S(2)}) collective-permute-start(f32[8,256]{1,0:T(8,128)S(1)} %pad_maximum_fusion.1), channel_id=1, source_target_pairs={{0,4},{1,5},{2,6},{3,7},{4,0},{5,1},{6,2},{7,3},{8,12},{9,13},{10,... | collective-permute-start | bytes 24584 | tf_op jit(solution)/shard_map/ppermute | solution.py:383
  9.3 1.6 %collective-permute-done.2 = f32[8,256]{1,0:T(8,128)S(1)} collective-permute-done((f32[8,256]{1,0:T(8,128)S(1)}, f32[8,256]{1,0:T(8,128)S(1)}, u32[]{:S(2)}, u32[]{:S(2)}) %collective-permute-start.2) | collective-permute-done | bytes 8224 | tf_op jit(solution)/shard_map/ppermute | solution.py:383
  11.0 3.1 %collective-permute-start.3 = (f32[16,256]{1,0:T(8,128)S(1)}, f32[16,256]{1,0:T(8,128)S(1)}, u32[]{:S(2)}, u32[]{:S(2)}) collective-permute-start(f32[16,256]{1,0:T(8,128)S(1)} %pad_maximum_fusion), channel_id=1, source_target_pairs={{0,8},{1,9},{2,10},{3,11},{4,12},{5,13},{6,14},{7,15},{8,0},{9,1},... | collective-permute-start | bytes 49160 | tf_op jit(solution)/shard_map/ppermute | solution.py:383
  14.1 0.1 pad_add_fusion.position_ref
  14.1 1.6 %collective-permute-done.3 = f32[16,256]{1,0:T(8,128)S(1)} collective-permute-done((f32[16,256]{1,0:T(8,128)S(1)}, f32[16,256]{1,0:T(8,128)S(1)}, u32[]{:S(2)}, u32[]{:S(2)}) %collective-permute-start.3) | collective-permute-done | bytes 16416 | tf_op jit(solution)/shard_map/ppermute | solution.py:383
  15.8 0.0 copy-start
  15.8 0.0 copy-start.4
  15.8 0.0 copy-start.5
  15.8 0.0 copy-start.1
  15.9 0.0 copy-start.2
  15.9 0.0 copy-start.3
  15.9 0.6 %copy-done = f32[8,128]{1,0:T(8,128)S(1)} copy-done((f32[8,128]{1,0:T(8,128)S(1)}, f32[8,128]{1,0:T(8,128)}, u32[]{:S(2)}) %copy-start) | copy-done | bytes 4120
  16.5 0.0 copy-done.4
  16.5 0.0 copy-done.5
  16.5 0.0 copy-done.1
  16.5 0.0 copy-done.2
  16.5 0.0 copy-done.3
  16.5 28.1 %shard_map.103 = (f32[2,128]{1,0:T(2,128)}, f32[2,128,128]{2,1,0:T(8,128)}, f32[2,128]{1,0:T(2,128)S(1)}) custom-call(s32[2]{0:T(128)S(1)} %pad_add_fusion.position_ref, f32[32,256]{1,0:T(8,128)S(1)} %concatenate.22.gathered_ref, f32[1,128]{1,0:T(1,128)S(1)} %bitcast.6, f32[1,128]{1,0:T(1,128)S(1)} %bitcast.7, f32[8,128]{1,0:T(8,128)S(1)} %copy-done, ...), custom_call_target="tpu_custom_call" | custom-call | tf_op jit(solution)/shard_map/pallas_call | solution.py:338
  44.7 0.6 %slice_reduce_fusion = f32[2]{0:T(128)} fusion(f32[2,128]{1,0:T(2,128)S(1)} %get-tuple-element.8), kind=kLoop, calls=%fused_computation.4 | loop fusion | bytes 16 | tf_op jit(solution)/shard_map/slice | solution.py:406
  (5 shorter events, 0.1 us)
Async XLA Ops:
  0.6 0.7 %copy-start.6 = (f32[2,128]{1,0:T(2,128)S(1)}, f32[2,128]{1,0:T(2,128)}, u32[]{:S(2)}) copy-start(f32[2,128]{1,0:T(2,128)} %param.8) | copy-start | bytes 3076
  1.3 1.3 %collective-permute-start = (f32[2,256]{1,0:T(2,128)S(1)}, f32[2,256]{1,0:T(2,128)S(1)}, u32[]{:S(2)}, u32[]{:S(2)}) collective-permute-start(f32[2,256]{1,0:T(2,128)S(1)} %pad_maximum_fusion.3), channel_id=1, source_target_pairs={{0,1},{1,0},{2,3},{3,2},{4,5},{5,4},{6,7},{7,6},{8,9},{9,8},{10,11... | collective-permute-start | bytes 6152 | tf_op jit(solution)/shard_map/ppermute | solution.py:383
  2.7 4.5 %collective-permute-start.1 = (f32[4,256]{1,0:T(4,128)S(1)}, f32[4,256]{1,0:T(4,128)S(1)}, u32[]{:S(2)}, u32[]{:S(2)}) collective-permute-start(f32[4,256]{1,0:T(4,128)S(1)} %pad_maximum_fusion.2), channel_id=1, source_target_pairs={{0,2},{1,3},{2,0},{3,1},{4,6},{5,7},{6,4},{7,5},{8,10},{9,11},{10,... | collective-permute-start | bytes 12296 | tf_op jit(solution)/shard_map/ppermute | solution.py:383
  7.2 3.8 %collective-permute-start.2 = (f32[8,256]{1,0:T(8,128)S(1)}, f32[8,256]{1,0:T(8,128)S(1)}, u32[]{:S(2)}, u32[]{:S(2)}) collective-permute-start(f32[8,256]{1,0:T(8,128)S(1)} %pad_maximum_fusion.1), channel_id=1, source_target_pairs={{0,4},{1,5},{2,6},{3,7},{4,0},{5,1},{6,2},{7,3},{8,12},{9,13},{10,... | collective-permute-start | bytes 24584 | tf_op jit(solution)/shard_map/ppermute | solution.py:383
  11.0 4.8 %collective-permute-start.3 = (f32[16,256]{1,0:T(8,128)S(1)}, f32[16,256]{1,0:T(8,128)S(1)}, u32[]{:S(2)}, u32[]{:S(2)}) collective-permute-start(f32[16,256]{1,0:T(8,128)S(1)} %pad_maximum_fusion), channel_id=1, source_target_pairs={{0,8},{1,9},{2,10},{3,11},{4,12},{5,13},{6,14},{7,15},{8,0},{9,1},... | collective-permute-start | bytes 49160 | tf_op jit(solution)/shard_map/ppermute | solution.py:383
  15.8 0.7 %copy-start = (f32[8,128]{1,0:T(8,128)S(1)}, f32[8,128]{1,0:T(8,128)}, u32[]{:S(2)}) copy-start(f32[8,128]{1,0:T(8,128)} %nw_ref.1) | copy-start | bytes 12292
  15.8 0.7 %copy-start.4 = (f32[128]{0:T(128)S(1)}, f32[128]{0:T(128)}, u32[]{:S(2)}) copy-start(f32[128]{0:T(128)} %param.14) | copy-start | bytes 1540
  15.8 0.7 %copy-start.5 = (f32[128]{0:T(128)S(1)}, f32[128]{0:T(128)}, u32[]{:S(2)}) copy-start(f32[128]{0:T(128)} %param.15) | copy-start | bytes 1540
  15.8 0.7 %copy-start.1 = (f32[128]{0:T(128)S(1)}, f32[128]{0:T(128)}, u32[]{:S(2)}) copy-start(f32[128]{0:T(128)} %param.10) | copy-start | bytes 1540
  15.9 0.7 %copy-start.2 = (f32[128]{0:T(128)S(1)}, f32[128]{0:T(128)}, u32[]{:S(2)}) copy-start(f32[128]{0:T(128)} %param.11) | copy-start | bytes 1540
  15.9 0.7 %copy-start.3 = (f32[128]{0:T(128)S(1)}, f32[128]{0:T(128)}, u32[]{:S(2)}) copy-start(f32[128]{0:T(128)} %param.13) | copy-start | bytes 1540

commit v2 on v1

--- a/solution.py
+++ b/solution.py
@@ -14,7 +14,7 @@
 LOG_TWO_PI = math.log(2.0 * math.pi)
 
 WINDOW = 4
-SLOTS = 48
+SLOTS = 32
 FAR = 1 << 29
 
 NN = (((1,), (0,)), ((), ()))

time: 45.5 us -> 39.8 us (0.87)
  Pallas kernels: 28.1 us -> 22 us
    pallas_call x1, Pallas kernels: 28.1 us -> 22 us  [chain(): pl.pallas_call(functools.partial(chain_kernel, own), out_shape=(jax.Shape...]
where the time goes in v2:
time: 39.8 us; the launch traced here: 39.2 us
  Pallas kernels  22 us (55%)
  starting transfers between devices  8.66 us (22%)
  waiting for transfers between devices  5.68 us (14%)
  local copies, waits for them, and re-layouts  1.34 us (3%)
  other arithmetic  0.79 us (2%)
  between operations  0.7 us (2%)
    pallas_call x1, Pallas kernels, chain(): pl.pallas_call(functools.partial(chain_kernel, own), out_shape=(jax.Shape...  22 us
    ppermute x4, starting transfers between devices, gather_all(): held = jnp.concatenate([held, lax.ppermute(held, axis, pairs)], axis=0)  8.66 us
    ppermute x4, waiting for transfers between devices, gather_all(): held = jnp.concatenate([held, lax.ppermute(held, axis, pairs)], axis=0)  5.68 us
  transfers between devices with their start and end apart: 4, of which 4 were waited for; matrix products, arithmetic and copies ran while one was open for 0% of the time, Pallas kernels for 0%

profile of v2, /device:TPU:0, one launch (start us, length us, event | category | flops | bytes accessed | tf_op | source)
XLA Modules:
  0.0 39.2 jit_solution(10166846928338227380)
XLA Ops:
  0.6 0.0 copy-start.6
  0.6 0.7 %convert_element_type.3 = f32[2,128]{1,0:T(2,128)S(1)} convert(s32[2,128]{1,0:T(2,128)} %param.9) | non-fusion elementwise | flops 256 | bytes 2048 | tf_op jit(solution)/shard_map/convert_element_type | solution.py:392
  1.3 0.0 copy-done.6
  1.3 0.5 %collective-permute-start = (f32[2,256]{1,0:T(2,128)S(1)}, f32[2,256]{1,0:T(2,128)S(1)}, u32[]{:S(2)}, u32[]{:S(2)}) collective-permute-start(f32[2,256]{1,0:T(2,128)S(1)} %pad_maximum_fusion.3), channel_id=1, source_target_pairs={{0,1},{1,0},{2,3},{3,2},{4,5},{5,4},{6,7},{7,6},{8,9},{9,8},{10,11... | collective-permute-start | bytes 6152 | tf_op jit(solution)/shard_map/ppermute | solution.py:383
  1.8 0.8 %collective-permute-done = f32[2,256]{1,0:T(2,128)S(1)} collective-permute-done((f32[2,256]{1,0:T(2,128)S(1)}, f32[2,256]{1,0:T(2,128)S(1)}, u32[]{:S(2)}, u32[]{:S(2)}) %collective-permute-start) | collective-permute-done | bytes 2080 | tf_op jit(solution)/shard_map/ppermute | solution.py:383
  2.7 2.9 %collective-permute-start.1 = (f32[4,256]{1,0:T(4,128)S(1)}, f32[4,256]{1,0:T(4,128)S(1)}, u32[]{:S(2)}, u32[]{:S(2)}) collective-permute-start(f32[4,256]{1,0:T(4,128)S(1)} %pad_maximum_fusion.2), channel_id=1, source_target_pairs={{0,2},{1,3},{2,0},{3,1},{4,6},{5,7},{6,4},{7,5},{8,10},{9,11},{10,... | collective-permute-start | bytes 12296 | tf_op jit(solution)/shard_map/ppermute | solution.py:383
  5.6 1.6 %collective-permute-done.1 = f32[4,256]{1,0:T(4,128)S(1)} collective-permute-done((f32[4,256]{1,0:T(4,128)S(1)}, f32[4,256]{1,0:T(4,128)S(1)}, u32[]{:S(2)}, u32[]{:S(2)}) %collective-permute-start.1) | collective-permute-done | bytes 4128 | tf_op jit(solution)/shard_map/ppermute | solution.py:383
  7.2 2.1 %collective-permute-start.2 = (f32[8,256]{1,0:T(8,128)S(1)}, f32[8,256]{1,0:T(8,128)S(1)}, u32[]{:S(2)}, u32[]{:S(2)}) collective-permute-start(f32[8,256]{1,0:T(8,128)S(1)} %pad_maximum_fusion.1), channel_id=1, source_target_pairs={{0,4},{1,5},{2,6},{3,7},{4,0},{5,1},{6,2},{7,3},{8,12},{9,13},{10,... | collective-permute-start | bytes 24584 | tf_op jit(solution)/shard_map/ppermute | solution.py:383
  9.3 1.6 %collective-permute-done.2 = f32[8,256]{1,0:T(8,128)S(1)} collective-permute-done((f32[8,256]{1,0:T(8,128)S(1)}, f32[8,256]{1,0:T(8,128)S(1)}, u32[]{:S(2)}, u32[]{:S(2)}) %collective-permute-start.2) | collective-permute-done | bytes 8224 | tf_op jit(solution)/shard_map/ppermute | solution.py:383
  11.0 3.1 %collective-permute-start.3 = (f32[16,256]{1,0:T(8,128)S(1)}, f32[16,256]{1,0:T(8,128)S(1)}, u32[]{:S(2)}, u32[]{:S(2)}) collective-permute-start(f32[16,256]{1,0:T(8,128)S(1)} %pad_maximum_fusion), channel_id=1, source_target_pairs={{0,8},{1,9},{2,10},{3,11},{4,12},{5,13},{6,14},{7,15},{8,0},{9,1},... | collective-permute-start | bytes 49160 | tf_op jit(solution)/shard_map/ppermute | solution.py:383
  14.1 0.1 pad_add_fusion.position_ref
  14.1 1.6 %collective-permute-done.3 = f32[16,256]{1,0:T(8,128)S(1)} collective-permute-done((f32[16,256]{1,0:T(8,128)S(1)}, f32[16,256]{1,0:T(8,128)S(1)}, u32[]{:S(2)}, u32[]{:S(2)}) %collective-permute-start.3) | collective-permute-done | bytes 16416 | tf_op jit(solution)/shard_map/ppermute | solution.py:383
  15.8 0.0 copy-start
  15.8 0.0 copy-start.4
  15.8 0.0 copy-start.5
  15.8 0.0 copy-start.1
  15.9 0.0 copy-start.2
  15.9 0.0 copy-start.3
  15.9 0.6 %copy-done = f32[8,128]{1,0:T(8,128)S(1)} copy-done((f32[8,128]{1,0:T(8,128)S(1)}, f32[8,128]{1,0:T(8,128)}, u32[]{:S(2)}) %copy-start) | copy-done | bytes 4120
  16.5 0.0 copy-done.4
  16.5 0.0 copy-done.5
  16.5 0.0 copy-done.1
  16.5 0.0 copy-done.2
  16.5 0.0 copy-done.3
  16.5 22.0 %shard_map.103 = (f32[2,128]{1,0:T(2,128)}, f32[2,128,128]{2,1,0:T(8,128)}, f32[2,128]{1,0:T(2,128)S(1)}) custom-call(s32[2]{0:T(128)S(1)} %pad_add_fusion.position_ref, f32[32,256]{1,0:T(8,128)S(1)} %concatenate.22.gathered_ref, f32[1,128]{1,0:T(1,128)S(1)} %bitcast.6, f32[1,128]{1,0:T(1,128)S(1)} %bitcast.7, f32[8,128]{1,0:T(8,128)S(1)} %copy-done, ...), custom_call_target="tpu_custom_call" | custom-call | tf_op jit(solution)/shard_map/pallas_call | solution.py:338
  38.6 0.6 %slice_reduce_fusion = f32[2]{0:T(128)} fusion(f32[2,128]{1,0:T(2,128)S(1)} %get-tuple-element.8), kind=kLoop, calls=%fused_computation.4 | loop fusion | bytes 16 | tf_op jit(solution)/shard_map/slice | solution.py:406
  (5 shorter events, 0.1 us)
Async XLA Ops:
  0.6 0.7 %copy-start.6 = (f32[2,128]{1,0:T(2,128)S(1)}, f32[2,128]{1,0:T(2,128)}, u32[]{:S(2)}) copy-start(f32[2,128]{1,0:T(2,128)} %param.8) | copy-start | bytes 3076
  1.3 1.3 %collective-permute-start = (f32[2,256]{1,0:T(2,128)S(1)}, f32[2,256]{1,0:T(2,128)S(1)}, u32[]{:S(2)}, u32[]{:S(2)}) collective-permute-start(f32[2,256]{1,0:T(2,128)S(1)} %pad_maximum_fusion.3), channel_id=1, source_target_pairs={{0,1},{1,0},{2,3},{3,2},{4,5},{5,4},{6,7},{7,6},{8,9},{9,8},{10,11... | collective-permute-start | bytes 6152 | tf_op jit(solution)/shard_map/ppermute | solution.py:383
  2.7 4.5 %collective-permute-start.1 = (f32[4,256]{1,0:T(4,128)S(1)}, f32[4,256]{1,0:T(4,128)S(1)}, u32[]{:S(2)}, u32[]{:S(2)}) collective-permute-start(f32[4,256]{1,0:T(4,128)S(1)} %pad_maximum_fusion.2), channel_id=1, source_target_pairs={{0,2},{1,3},{2,0},{3,1},{4,6},{5,7},{6,4},{7,5},{8,10},{9,11},{10,... | collective-permute-start | bytes 12296 | tf_op jit(solution)/shard_map/ppermute | solution.py:383
  7.2 3.8 %collective-permute-start.2 = (f32[8,256]{1,0:T(8,128)S(1)}, f32[8,256]{1,0:T(8,128)S(1)}, u32[]{:S(2)}, u32[]{:S(2)}) collective-permute-start(f32[8,256]{1,0:T(8,128)S(1)} %pad_maximum_fusion.1), channel_id=1, source_target_pairs={{0,4},{1,5},{2,6},{3,7},{4,0},{5,1},{6,2},{7,3},{8,12},{9,13},{10,... | collective-permute-start | bytes 24584 | tf_op jit(solution)/shard_map/ppermute | solution.py:383
  11.0 4.8 %collective-permute-start.3 = (f32[16,256]{1,0:T(8,128)S(1)}, f32[16,256]{1,0:T(8,128)S(1)}, u32[]{:S(2)}, u32[]{:S(2)}) collective-permute-start(f32[16,256]{1,0:T(8,128)S(1)} %pad_maximum_fusion), channel_id=1, source_target_pairs={{0,8},{1,9},{2,10},{3,11},{4,12},{5,13},{6,14},{7,15},{8,0},{9,1},... | collective-permute-start | bytes 49160 | tf_op jit(solution)/shard_map/ppermute | solution.py:383
  15.8 0.7 %copy-start = (f32[8,128]{1,0:T(8,128)S(1)}, f32[8,128]{1,0:T(8,128)}, u32[]{:S(2)}) copy-start(f32[8,128]{1,0:T(8,128)} %nw_ref.1) | copy-start | bytes 12292
  15.8 0.7 %copy-start.4 = (f32[128]{0:T(128)S(1)}, f32[128]{0:T(128)}, u32[]{:S(2)}) copy-start(f32[128]{0:T(128)} %param.14) | copy-start | bytes 1540
  15.8 0.7 %copy-start.5 = (f32[128]{0:T(128)S(1)}, f32[128]{0:T(128)}, u32[]{:S(2)}) copy-start(f32[128]{0:T(128)} %param.15) | copy-start | bytes 1540
  15.8 0.7 %copy-start.1 = (f32[128]{0:T(128)S(1)}, f32[128]{0:T(128)}, u32[]{:S(2)}) copy-start(f32[128]{0:T(128)} %param.10) | copy-start | bytes 1540
  15.9 0.7 %copy-start.2 = (f32[128]{0:T(128)S(1)}, f32[128]{0:T(128)}, u32[]{:S(2)}) copy-start(f32[128]{0:T(128)} %param.11) | copy-start | bytes 1540
  15.9 0.7 %copy-start.3 = (f32[128]{0:T(128)S(1)}, f32[128]{0:T(128)}, u32[]{:S(2)}) copy-start(f32[128]{0:T(128)} %param.13) | copy-start | bytes 1540

commit v3 on v2

--- a/solution.py
+++ b/solution.py
@@ -46,17 +46,6 @@
 def dot(left, right, dims=NN):
     (left_axis,), (right_axis,) = dims[0]
     return raw(as_left(left, left_axis), as_right(right, right_axis), dims)
-
-
-def exact_dot(ones_left, right, dims=NN):
-    (left_axis,), (right_axis,) = dims[0]
-    high, low = halves(right)
-    left = ones_left.astype(BF)
-    return raw(
-        jnp.concatenate([left, left], axis=left_axis),
-        jnp.concatenate([high, low], axis=right_axis),
-        dims,
-    )
 
 
 def iota(shape, axis):
@@ -118,16 +107,48 @@
     return sides, pivots, quad[7:8, :]
 
 
+def tables_kernel(
+    nw_ref, damping_ref, process_ref, noise_ref, mean_ref, var_ref, strip_ref, big_ref, added_ref, line_ref
+):
+    size = GX * GY
+    process = process_ref[...]
+    line_ref[...] = jnp.concatenate(
+        [mean_ref[...], var_ref[...], process, noise_ref[...], jnp.zeros((4, size), F32)], axis=0
+    )
+    powers = [
+        (iota((size, size), 0) == iota((size, size), 1)).astype(F32),
+        transition(nw_ref[...], damping_ref[...]),
+    ]
+    for e in range(2, WINDOW + 1):
+        powers.append(dot(powers[(e + 1) // 2], powers[e // 2]))
+    band = 3 * size
+    strip_ref[...] = jnp.zeros_like(strip_ref)
+    for e in range(WINDOW + 1):
+        at = (WINDOW - e) * band
+        strip_ref[:, at : at + band] = as_right(powers[e], 1)
+    added_ref[0] = jnp.zeros((size, size), F32)
+    added = jnp.zeros((size, size), F32)
+    for e in range(1, WINDOW + 1):
+        added = added + dot(powers[e - 1] * process, powers[e - 1], NT)
+        added_ref[e] = added
+    big_ref[...] = jnp.zeros_like(big_ref)
+    wide = (WINDOW - 1) * size
+    for i in range(1, WINDOW):
+        for l in range(0, i):
+            high, low = halves(powers[i - l])
+            for piece, held in enumerate((high, low)):
+                start = piece * wide + (i - 1) * size
+                big_ref[start : start + size, l * size : (l + 1) * size] = held
+
+
 def chain_kernel(
     own,
     position_ref,
     gathered_ref,
-    mean_ref,
-    var_ref,
-    nw_ref,
-    damping_ref,
-    process_ref,
-    noise_ref,
+    strip_ref,
+    big_ref,
+    added_ref,
+    line_ref,
     smooth_mean_ref,
     smooth_cov_ref,
     loglik_ref,
@@ -136,12 +157,9 @@
     rank_s,
     off_v,
     off_s,
-    power_s,
-    left_s,
-    right_s,
-    big_s,
-    psi_s,
-    added_s,
+    watch_s,
+    fixed_s,
+    noise_s,
     cov_s,
     trans_s,
     info_s,
@@ -160,8 +178,7 @@
     padded = mask_s.shape[0]
     position = position_ref[0]
     base = position * own
-    nw, damping = nw_ref[...], damping_ref[...]
-    process, noise = process_ref[...], noise_ref[...]
+    process, noise = line_ref[2:3, :], line_ref[3:4, :]
 
     mask_s[...] = jnp.zeros_like(mask_s)
     obs_s[...] = jnp.zeros_like(obs_s)
@@ -186,33 +203,9 @@
     rank_s[...] = jnp.where(mask > 0.0, rank.astype(jnp.int32), FAR)
 
     eye = (iota((size, size), 0) == iota((size, size), 1)).astype(F32)
-    power_s[0] = eye
-    power_s[1] = transition(nw, damping)
-    for e in range(2, WINDOW + 1):
-        power_s[e] = dot(power_s[(e + 1) // 2], power_s[e // 2])
-    psi_s[...] = jnp.zeros_like(psi_s)
-    big_s[...] = jnp.zeros_like(big_s)
-    added_s[0] = jnp.zeros((size, size), F32)
-    wide = (WINDOW - 1) * size
-    for e in range(WINDOW + 1):
-        left_s[e] = as_left(power_s[e], 1)
-        right_s[e] = as_right(power_s[e], 1)
-        if e >= 1:
-            moved = power_s[e - 1]
-            added_s[e] = added_s[e - 1] + dot(moved * process, moved, NT)
-        for l in range(1, min(e, WINDOW - 1) + 1):
-            high, low = halves(power_s[e - l])
-            for piece, held in enumerate((high, low, high)):
-                psi_s[e, :, piece * wide + (l - 1) * size : piece * wide + l * size] = held
-    for i in range(1, WINDOW):
-        for l in range(0, i):
-            high, low = halves(power_s[i - l])
-            for piece, held in enumerate((high, low)):
-                start = piece * wide + (i - 1) * size
-                big_s[start : start + size, l * size : (l + 1) * size] = held
-
-    cov_s[...] = eye * var_ref[...]
-    mean_s[...] = mean_ref[...]
+    band = 3 * size
+    cov_s[...] = eye * line_ref[1:2, :]
+    mean_s[...] = line_ref[0:1, :]
     trans_s[...] = jnp.zeros_like(trans_s)
     info_s[...] = jnp.zeros_like(info_s)
     pull_s[...] = jnp.zeros_like(pull_s)
@@ -220,48 +213,43 @@
     copy.wait()
     last_row = iota((SLOTS, 1), 0) == SLOTS - 1
 
-    def body(state):
-        step, first = state
-        inside = (step >= base) & (step < base + own)
-        cut = jnp.where(step < base, base, jnp.where(inside, step + 1, steps))
+    def is_own(step):
+        return (step >= base) & (step < base + own)
+
+    def extent(step, first):
+        cut = jnp.where(step < base, base, jnp.where(is_own(step), step + 1, steps))
         end = jnp.minimum(step + WINDOW, cut)
         taken = jnp.minimum(off_s[0, end] - first, SLOTS - 1)
         ahead = jnp.int32(0)
         for i in range(1, WINDOW + 1):
             done = (step + i <= end) & (off_s[0, step + i] <= first + taken)
             ahead = ahead + done.astype(jnp.int32)
-        mine = jnp.clip(step - base, 0, own - 1)
-
-        @pl.when(inside & (first == off_s[0, step]))
-        def _():
-            kept_cov[mine] = cov_s[...]
-            kept_mean[mine] = mean_s[...]
-            kept_trans[mine] = trans_s[...]
-            kept_info[mine] = info_s[...]
-            kept_pull[mine] = pull_s[...]
-            trans_s[...] = eye
-            info_s[...] = jnp.zeros_like(info_s)
-            pull_s[...] = jnp.zeros_like(pull_s)
-
+        return taken, ahead
+
+    def power(e, count=1):
+        return strip_ref[:, pl.ds(pl.multiple_of((WINDOW - e) * band, band), count * band)]
+
+    def prepare(step, first, taken, ahead):
         slot = iota((SLOTS, size), 0)
         picks = []
         for i in range(WINDOW):
             where = rank_s[pl.ds(step + i, 1), :] - first
             picks.append(jnp.where((slot == where) & (slot < taken), 1.0, 0.0))
         tail = jnp.concatenate(picks[1:], axis=1).astype(BF)
-        spread_out = raw(jnp.concatenate([tail, tail], axis=1), big_s[...], NN)
-        watch = picks[0] + spread_out[:, :size]
-        shocks = jnp.concatenate(
-            [
-                picks[l] + (spread_out[:, l * size : (l + 1) * size] if l < WINDOW - 1 else 0.0)
-                for l in range(1, WINDOW)
-            ],
-            axis=1,
-        )
-        scaled = shocks * jnp.concatenate([process] * (WINDOW - 1), axis=1)
+        spread_out = raw(jnp.concatenate([tail, tail], axis=1), big_ref[...], NN)
+        watch = as_right(picks[0] + spread_out[:, :size], 1)
+        lefts, rights = [], []
+        for l in range(1, WINDOW):
+            shock = picks[l]
+            if l < WINDOW - 1:
+                shock = shock + spread_out[:, l * size : (l + 1) * size]
+            lefts.append(as_left(shock * process, 1))
+            rights.append(as_right(shock, 1))
         fixed = raw(
-            as_left(scaled, 1),
-            jnp.concatenate([as_right(shocks, 1), psi_s[ahead]], axis=0),
+            jnp.concatenate(lefts, axis=1),
+            jnp.concatenate(
+                [jnp.concatenate(rights, axis=1), power(ahead - 1, WINDOW - 1)], axis=0
+            ),
             NT,
         )
         readings = jnp.concatenate(
@@ -282,22 +270,45 @@
         diagonal = (iota((SLOTS, SLOTS), 0) == iota((SLOTS, SLOTS), 1)) & (
             iota((SLOTS, SLOTS), 0) >= taken
         )
-        own_noise = own_noise + diagonal.astype(F32)
-
-        cov, trans = cov_s[...], trans_s[...]
-        cov_right, trans_right = as_right(cov, 0), as_right(trans, 0)
-        seen = raw(as_left(watch, 1), jnp.concatenate([cov_right, trans_right], axis=1), NN)
+        return watch, fixed[:, SLOTS:], fixed[:, :SLOTS] + own_noise + diagonal.astype(F32)
+
+    zero = jnp.int32(0)
+    opening = extent(zero, zero)
+    watch_s[...], fixed_s[...], noise_s[...] = prepare(zero, zero, *opening)
+
+    def body(state):
+        step, first, taken, ahead = state
+        inside = is_own(step)
+        mine = jnp.clip(step - base, 0, own - 1)
+
+        @pl.when(inside & (first == off_s[0, step]))
+        def _():
+            kept_cov[mine] = cov_s[...]
+            kept_mean[mine] = mean_s[...]
+            kept_trans[mine] = trans_s[...]
+            kept_info[mine] = info_s[...]
+            kept_pull[mine] = pull_s[...]
+            trans_s[...] = eye
+            info_s[...] = jnp.zeros_like(info_s)
+            pull_s[...] = jnp.zeros_like(pull_s)
+
+        both = as_left(jnp.concatenate([cov_s[...], trans_s[...]], axis=1), 0)
+        watch = watch_s[...]
+        seen = raw(watch, both, NN)
         seen_cov = jnp.where(last_row, mean_s[...], seen[:, :size])
         seen_trans = jnp.where(last_row, pull_s[...], seen[:, size:])
-        joint = fixed + raw(
-            as_left(seen_cov, 1),
-            jnp.concatenate([as_right(watch, 1), right_s[ahead]], axis=0),
-            NT,
-        )
-        moved = raw(left_s[ahead], jnp.concatenate([cov_right, trans_right], axis=1), NN)
-        moved_cov = raw(as_left(moved[:, :size], 1), right_s[ahead], NT) + added_s[ahead]
-        square = joint[:, :SLOTS] + own_noise
-        (to_state, to_trans), pivots, quad = eliminate(square, (joint[:, SLOTS:], seen_trans))
+        moving = power(ahead)
+        joint = raw(as_left(seen_cov, 1), jnp.concatenate([watch, moving], axis=0), NT)
+        square = joint[:, :SLOTS] + noise_s[...]
+        side = joint[:, SLOTS:] + fixed_s[...]
+        moved = raw(moving, both, NN)
+        moved_cov = raw(as_left(moved[:, :size], 1), moving, NT) + added_ref[ahead]
+
+        next_step, next_first = step + ahead, first + taken
+        following = extent(next_step, next_first)
+        prepared = prepare(next_step, next_first, *following)
+
+        (to_state, to_trans), pivots, quad = eliminate(square, (side, seen_trans))
         mean_s[...] = to_state[SLOTS - 1 :, :]
         pull_s[...] = to_trans[SLOTS - 1 :, :]
         scale = jnp.where(last_row, 0.0, lax.rsqrt(pivots))
@@ -306,6 +317,7 @@
         cov_s[...] = moved_cov - outer[:size, :size]
         trans_s[...] = moved[:, size:] - outer[:size, size:]
         info_s[...] = info_s[...] + outer[size:, size:]
+        watch_s[...], fixed_s[...], noise_s[...] = prepared
 
         @pl.when(inside)
         def _():
@@ -313,49 +325,66 @@
             count = taken.astype(F32) * LOG_TWO_PI
             kept_lik[mine] = kept_lik[mine] + (log_det + quad + count)
 
-        return step + ahead, first + taken
-
-    lax.while_loop(lambda state: state[0] < steps, body, (jnp.int32(0), jnp.int32(0)))
+        return (next_step, next_first) + following
+
+    lax.while_loop(lambda state: state[0] < steps, body, (zero, zero) + opening)
 
     info, pull = info_s[...], pull_s[...]
     for j in range(own - 1, -1, -1):
         cov = kept_cov[j]
         smooth_cov_ref[j] = cov - dot(dot(cov, info), cov)
         smooth_mean_ref[j : j + 1, :] = kept_mean[j] + dot(pull, cov)
-        loglik_ref[j : j + 1, :] = kept_lik[j] * (-1.0 / (2.0 * size))
+        loglik_ref[:, j : j + 1] = kept_lik[j][:, :1] * (-1.0 / (2.0 * size))
         if j > 0:
             trans = kept_trans[j]
             info = kept_info[j] + dot(dot(trans, info, TN), trans)
             pull = kept_pull[j] + dot(pull, trans)
 
 
-def chain(position, gathered, prior_mean, prior_var, nw, damping, process_var, obs_var, own):
+VMEM = pl.BlockSpec(memory_space=pltpu.VMEM)
+LIMIT = 48 * 1024 * 1024
+
+
+def tables(nw, damping, process_var, obs_var, prior_mean, prior_var):
+    size = nw.shape[1]
+    wide = (WINDOW - 1) * size
+    return pl.pallas_call(
+        tables_kernel,
+        out_shape=(
+            jax.ShapeDtypeStruct((size, 2 * WINDOW * 3 * size), BF),
+            jax.ShapeDtypeStruct((2 * wide, wide), BF),
+            jax.ShapeDtypeStruct((WINDOW + 1, size, size), F32),
+            jax.ShapeDtypeStruct((8, size), F32),
+        ),
+        in_specs=[VMEM] * 6,
+        out_specs=(VMEM,) * 4,
+        compiler_params=pltpu.CompilerParams(vmem_limit_bytes=LIMIT),
+        cost_estimate=pl.CostEstimate(flops=10**8, bytes_accessed=2 * 10**6, transcendentals=0),
+    )(nw, damping, process_var, obs_var, prior_mean, prior_var)
+
+
+def chain(position, gathered, strip, big, added, line, own):
     steps, size = gathered.shape[0], gathered.shape[1] // 2
     padded = -(-(steps + WINDOW + 1) // 128) * 128
-    wide = (WINDOW - 1) * size
-    vmem = pl.BlockSpec(memory_space=pltpu.VMEM)
     square = (size, size)
     return pl.pallas_call(
         functools.partial(chain_kernel, own),
         out_shape=(
             jax.ShapeDtypeStruct((own, size), F32),
             jax.ShapeDtypeStruct((own, size, size), F32),
-            jax.ShapeDtypeStruct((own, size), F32),
+            jax.ShapeDtypeStruct((1, own), F32),
         ),
-        in_specs=[pl.BlockSpec(memory_space=pltpu.SMEM)] + [vmem] * 7,
-        out_specs=(vmem, vmem, vmem),
+        in_specs=[pl.BlockSpec(memory_space=pltpu.SMEM)] + [VMEM] * 5,
+        out_specs=(VMEM,) * 3,
         scratch_shapes=[
             pltpu.VMEM((padded, size), F32),
             pltpu.VMEM((padded, size), F32),
             pltpu.VMEM((padded, size), jnp.int32),
             pltpu.VMEM((8, padded), jnp.int32),
             pltpu.SMEM((8, padded), jnp.int32),
-            pltpu.VMEM((WINDOW + 1,) + square, F32),
-            pltpu.VMEM((WINDOW + 1, size, 3 * size), BF),
-            pltpu.VMEM((WINDOW + 1, size, 3 * size), BF),
-            pltpu.VMEM((2 * wide, wide), BF),
-            pltpu.VMEM((WINDOW + 1, size, 3 * wide), BF),
-            pltpu.VMEM((WINDOW + 1,) + square, F32),
+            pltpu.VMEM((SLOTS, 3 * size), BF),
+            pltpu.VMEM((SLOTS, size), F32),
+            pltpu.VMEM((SLOTS, SLOTS), F32),
             pltpu.VMEM(square, F32),
             pltpu.VMEM(square, F32),
             pltpu.VMEM(square, F32),
@@ -369,8 +398,8 @@
             pltpu.VMEM((own, 1, size), F32),
             pltpu.SemaphoreType.DMA(()),
         ],
-        compiler_params=pltpu.CompilerParams(vmem_limit_bytes=48 * 1024 * 1024),
-    )(position, gathered, prior_mean, prior_var, nw, damping, process_var, obs_var)
+        compiler_params=pltpu.CompilerParams(vmem_limit_bytes=LIMIT),
+    )(position, gathered, strip, big, added, line)
 
 
 def gather_all(block, axis):
@@ -392,18 +421,11 @@
     block = jnp.concatenate([observed, obs_mask.astype(F32)], axis=1)
     gathered, flip = gather_all(block, "tm")
     position = jnp.stack([lax.axis_index("tm").astype(jnp.int32), flip])
-    smooth_mean, smooth_cov, loglik = chain(
-        position,
-        gathered,
-        prior_mean[None],
-        prior_var[None],
-        neighbor_weights,
-        damping[None],
-        process_var[None],
-        obs_var[None],
-        own,
+    made = tables(
+        neighbor_weights, damping[None], process_var[None], obs_var[None], prior_mean[None], prior_var[None]
     )
-    return smooth_mean, smooth_cov, loglik[:, 0]
+    smooth_mean, smooth_cov, loglik = chain(position, gathered, *made, own)
+    return smooth_mean, smooth_cov, loglik.reshape(own)
 
 
 def solution(mesh):

time: 39.8 us -> 35 us (0.88)
  Pallas kernels: 22 us -> 19.4 us
  waiting for transfers between devices: 5.68 us -> 4.26 us
  local copies, waits for them, and re-layouts: 1.34 us -> 0.74 us
    pallas_call x1, Pallas kernels: 22 us -> 18.7 us  [chain(): pl.pallas_call(functools.partial(chain_kernel, own), out_shape=(jax.Shape...]
    ppermute x4, waiting for transfers between devices: 5.68 us -> 4.26 us  [gather_all(): held = jnp.concatenate([held, lax.ppermute(held, axis, pairs)], axis=0)]
    pallas_call x0 -> x1, Pallas kernels: none -> 0.68 us  [tables(): pl.pallas_call(tables_kernel, out_shape=(jax.ShapeDtypeStruct((size, 2 *...]
    slice x1 -> x0, local copies, waits for them, and re-layouts: 0.63 us -> none  [local(): return (smooth_mean, smooth_cov, loglik[:, 0])]
  transfers between devices with their start and end apart: 4 -> 4, of which waited for: 4 -> 4; matrix products, arithmetic and copies ran while one was open for 0% -> 0% of each run, Pallas kernels for 0% -> 2%
where the time goes in v3:
time: 35 us; the launch traced here: 34.5 us
  Pallas kernels  19.4 us (55%)
  starting transfers between devices  8.66 us (25%)
  waiting for transfers between devices  4.26 us (12%)
  other arithmetic  0.79 us (2%)
  local copies, waits for them, and re-layouts  0.74 us (2%)
  between operations  0.68 us (2%)
    pallas_call x1, Pallas kernels, chain(): pl.pallas_call(functools.partial(chain_kernel, own), out_shape=(jax.Shape...  18.7 us
    ppermute x4, starting transfers between devices, gather_all(): held = jnp.concatenate([held, lax.ppermute(held, axis, pairs)], axis=0)  8.66 us
    ppermute x4, waiting for transfers between devices, gather_all(): held = jnp.concatenate([held, lax.ppermute(held, axis, pairs)], axis=0)  4.26 us
    unnamed x14, local copies, waits for them, and re-layouts  0.72 us
  transfers between devices with their start and end apart: 4, of which 4 were waited for; matrix products, arithmetic and copies ran while one was open for 0% of the time, Pallas kernels for 2%

profile of v3, /device:TPU:0, one launch (start us, length us, event | category | flops | bytes accessed | tf_op | source)
XLA Modules:
  0.0 34.5 jit_solution(5732032963318966309)
XLA Ops:
  0.6 0.0 copy-start.6
  0.6 0.7 %convert_element_type.3 = f32[2,128]{1,0:T(2,128)S(1)} convert(s32[2,128]{1,0:T(2,128)} %param.9) | non-fusion elementwise | flops 256 | bytes 2048 | tf_op jit(solution)/shard_map/convert_element_type | solution.py:421
  1.3 0.0 copy-done.6
  1.3 0.5 %collective-permute-start = (f32[2,256]{1,0:T(2,128)S(1)}, f32[2,256]{1,0:T(2,128)S(1)}, u32[]{:S(2)}, u32[]{:S(2)}) collective-permute-start(f32[2,256]{1,0:T(2,128)S(1)} %pad_maximum_fusion.3), channel_id=1, source_target_pairs={{0,1},{1,0},{2,3},{3,2},{4,5},{5,4},{6,7},{7,6},{8,9},{9,8},{10,11... | collective-permute-start | bytes 6152 | tf_op jit(solution)/shard_map/ppermute | solution.py:412
  1.8 0.8 %collective-permute-done = f32[2,256]{1,0:T(2,128)S(1)} collective-permute-done((f32[2,256]{1,0:T(2,128)S(1)}, f32[2,256]{1,0:T(2,128)S(1)}, u32[]{:S(2)}, u32[]{:S(2)}) %collective-permute-start) | collective-permute-done | bytes 2080 | tf_op jit(solution)/shard_map/ppermute | solution.py:412
  2.7 2.9 %collective-permute-start.1 = (f32[4,256]{1,0:T(4,128)S(1)}, f32[4,256]{1,0:T(4,128)S(1)}, u32[]{:S(2)}, u32[]{:S(2)}) collective-permute-start(f32[4,256]{1,0:T(4,128)S(1)} %pad_maximum_fusion.2), channel_id=1, source_target_pairs={{0,2},{1,3},{2,0},{3,1},{4,6},{5,7},{6,4},{7,5},{8,10},{9,11},{10,... | collective-permute-start | bytes 12296 | tf_op jit(solution)/shard_map/ppermute | solution.py:412
  5.6 1.6 %collective-permute-done.1 = f32[4,256]{1,0:T(4,128)S(1)} collective-permute-done((f32[4,256]{1,0:T(4,128)S(1)}, f32[4,256]{1,0:T(4,128)S(1)}, u32[]{:S(2)}, u32[]{:S(2)}) %collective-permute-start.1) | collective-permute-done | bytes 4128 | tf_op jit(solution)/shard_map/ppermute | solution.py:412
  7.2 2.1 %collective-permute-start.2 = (f32[8,256]{1,0:T(8,128)S(1)}, f32[8,256]{1,0:T(8,128)S(1)}, u32[]{:S(2)}, u32[]{:S(2)}) collective-permute-start(f32[8,256]{1,0:T(8,128)S(1)} %pad_maximum_fusion.1), channel_id=1, source_target_pairs={{0,4},{1,5},{2,6},{3,7},{4,0},{5,1},{6,2},{7,3},{8,12},{9,13},{10,... | collective-permute-start | bytes 24584 | tf_op jit(solution)/shard_map/ppermute | solution.py:412
  9.3 1.6 %collective-permute-done.2 = f32[8,256]{1,0:T(8,128)S(1)} collective-permute-done((f32[8,256]{1,0:T(8,128)S(1)}, f32[8,256]{1,0:T(8,128)S(1)}, u32[]{:S(2)}, u32[]{:S(2)}) %collective-permute-start.2) | collective-permute-done | bytes 8224 | tf_op jit(solution)/shard_map/ppermute | solution.py:412
  11.0 3.1 %collective-permute-start.3 = (f32[16,256]{1,0:T(8,128)S(1)}, f32[16,256]{1,0:T(8,128)S(1)}, u32[]{:S(2)}, u32[]{:S(2)}) collective-permute-start(f32[16,256]{1,0:T(8,128)S(1)} %pad_maximum_fusion), channel_id=1, source_target_pairs={{0,8},{1,9},{2,10},{3,11},{4,12},{5,13},{6,14},{7,15},{8,0},{9,1},... | collective-permute-start | bytes 49160 | tf_op jit(solution)/shard_map/ppermute | solution.py:412
  14.1 0.1 pad_add_fusion.position_ref
  14.1 0.0 copy-start
  14.1 0.0 copy-start.4
  14.2 0.0 copy-start.5
  14.2 0.0 copy-start.1
  14.2 0.0 copy-start.2
  14.2 0.0 copy-start.3
  14.2 0.7 %copy-done = f32[8,128]{1,0:T(8,128)S(1)} copy-done((f32[8,128]{1,0:T(8,128)S(1)}, f32[8,128]{1,0:T(8,128)}, u32[]{:S(2)}) %copy-start) | copy-done | bytes 4120
  14.8 0.0 copy-done.4
  14.8 0.0 copy-done.5
  14.8 0.0 copy-done.1
  14.8 0.0 copy-done.2
  14.9 0.0 copy-done.3
  14.9 0.7 %shard_map.103 = (bf16[128,3072]{1,0:T(8,128)(2,1)S(1)}, bf16[768,384]{1,0:T(8,128)(2,1)S(1)}, f32[5,128,128]{2,1,0:T(8,128)S(1)}, f32[8,128]{1,0:T(8,128)S(1)}) custom-call(f32[8,128]{1,0:T(8,128)S(1)} %copy-done, f32[1,128]{1,0:T(1,128)S(1)} %bitcast.7, f32[1,128]{1,0:T(1,128)S(1)} %bitcast.8, f32[1,128]{1,0:T(1,128)S(1)} %bitcast.9, ...), custom_call_target="tpu_custom_call" | custom-call | flops 100000000 | bytes 2000000 | tf_op jit(solution)/shard_map/pallas_call | solution.py:351
  15.6 0.2 collective-permute-done.3
  15.8 18.7 %shard_map.104 = (f32[2,128]{1,0:T(2,128)}, f32[2,128,128]{2,1,0:T(8,128)}, f32[1,2]{1,0:T(1,128)}) custom-call(s32[2]{0:T(128)S(1)} %pad_add_fusion.position_ref, f32[32,256]{1,0:T(8,128)S(1)} %concatenate.22.gathered_ref, bf16[128,3072]{1,0:T(8,128)(2,1)S(1)} %get-tuple-element.10.strip_ref, bf16[768,384]{1,0:T(8,128)(2,1)S(1)} %get-tuple-element.11.big_ref, ...), custom_call_target="tpu_custom_call" | custom-call | tf_op jit(solution)/shard_map/pallas_call | solution.py:370
  (5 shorter events, 0.1 us)
Async XLA Ops:
  0.6 0.7 %copy-start.6 = (f32[2,128]{1,0:T(2,128)S(1)}, f32[2,128]{1,0:T(2,128)}, u32[]{:S(2)}) copy-start(f32[2,128]{1,0:T(2,128)} %param.8) | copy-start | bytes 3076
  1.3 1.3 %collective-permute-start = (f32[2,256]{1,0:T(2,128)S(1)}, f32[2,256]{1,0:T(2,128)S(1)}, u32[]{:S(2)}, u32[]{:S(2)}) collective-permute-start(f32[2,256]{1,0:T(2,128)S(1)} %pad_maximum_fusion.3), channel_id=1, source_target_pairs={{0,1},{1,0},{2,3},{3,2},{4,5},{5,4},{6,7},{7,6},{8,9},{9,8},{10,11... | collective-permute-start | bytes 6152 | tf_op jit(solution)/shard_map/ppermute | solution.py:412
  2.7 4.5 %collective-permute-start.1 = (f32[4,256]{1,0:T(4,128)S(1)}, f32[4,256]{1,0:T(4,128)S(1)}, u32[]{:S(2)}, u32[]{:S(2)}) collective-permute-start(f32[4,256]{1,0:T(4,128)S(1)} %pad_maximum_fusion.2), channel_id=1, source_target_pairs={{0,2},{1,3},{2,0},{3,1},{4,6},{5,7},{6,4},{7,5},{8,10},{9,11},{10,... | collective-permute-start | bytes 12296 | tf_op jit(solution)/shard_map/ppermute | solution.py:412
  7.2 3.8 %collective-permute-start.2 = (f32[8,256]{1,0:T(8,128)S(1)}, f32[8,256]{1,0:T(8,128)S(1)}, u32[]{:S(2)}, u32[]{:S(2)}) collective-permute-start(f32[8,256]{1,0:T(8,128)S(1)} %pad_maximum_fusion.1), channel_id=1, source_target_pairs={{0,4},{1,5},{2,6},{3,7},{4,0},{5,1},{6,2},{7,3},{8,12},{9,13},{10,... | collective-permute-start | bytes 24584 | tf_op jit(solution)/shard_map/ppermute | solution.py:412
  11.0 4.8 %collective-permute-start.3 = (f32[16,256]{1,0:T(8,128)S(1)}, f32[16,256]{1,0:T(8,128)S(1)}, u32[]{:S(2)}, u32[]{:S(2)}) collective-permute-start(f32[16,256]{1,0:T(8,128)S(1)} %pad_maximum_fusion), channel_id=1, source_target_pairs={{0,8},{1,9},{2,10},{3,11},{4,12},{5,13},{6,14},{7,15},{8,0},{9,1},... | collective-permute-start | bytes 49160 | tf_op jit(solution)/shard_map/ppermute | solution.py:412
  14.1 0.7 %copy-start = (f32[8,128]{1,0:T(8,128)S(1)}, f32[8,128]{1,0:T(8,128)}, u32[]{:S(2)}) copy-start(f32[8,128]{1,0:T(8,128)} %nw_ref.1) | copy-start | bytes 12292
  14.1 0.7 %copy-start.4 = (f32[128]{0:T(128)S(1)}, f32[128]{0:T(128)}, u32[]{:S(2)}) copy-start(f32[128]{0:T(128)} %param.10) | copy-start | bytes 1540
  14.2 0.7 %copy-start.5 = (f32[128]{0:T(128)S(1)}, f32[128]{0:T(128)}, u32[]{:S(2)}) copy-start(f32[128]{0:T(128)} %param.11) | copy-start | bytes 1540
  14.2 0.7 %copy-start.1 = (f32[128]{0:T(128)S(1)}, f32[128]{0:T(128)}, u32[]{:S(2)}) copy-start(f32[128]{0:T(128)} %param.13) | copy-start | bytes 1540
  14.2 0.7 %copy-start.2 = (f32[128]{0:T(128)S(1)}, f32[128]{0:T(128)}, u32[]{:S(2)}) copy-start(f32[128]{0:T(128)} %param.14) | copy-start | bytes 1540
  14.2 0.7 %copy-start.3 = (f32[128]{0:T(128)S(1)}, f32[128]{0:T(128)}, u32[]{:S(2)}) copy-start(f32[128]{0:T(128)} %param.15) | copy-start | bytes 1540

commit v4 on v3

--- a/solution.py
+++ b/solution.py
@@ -131,14 +131,10 @@
     for e in range(1, WINDOW + 1):
         added = added + dot(powers[e - 1] * process, powers[e - 1], NT)
         added_ref[e] = added
-    big_ref[...] = jnp.zeros_like(big_ref)
-    wide = (WINDOW - 1) * size
     for i in range(1, WINDOW):
-        for l in range(0, i):
-            high, low = halves(powers[i - l])
-            for piece, held in enumerate((high, low)):
-                start = piece * wide + (i - 1) * size
-                big_ref[start : start + size, l * size : (l + 1) * size] = held
+        high, low = halves(powers[i])
+        big_ref[:size, (i - 1) * size : i * size] = high
+        big_ref[size:, (i - 1) * size : i * size] = low
 
 
 def chain_kernel(
@@ -235,14 +231,18 @@
         for i in range(WINDOW):
             where = rank_s[pl.ds(step + i, 1), :] - first
             picks.append(jnp.where((slot == where) & (slot < taken), 1.0, 0.0))
-        tail = jnp.concatenate(picks[1:], axis=1).astype(BF)
-        spread_out = raw(jnp.concatenate([tail, tail], axis=1), big_ref[...], NN)
-        watch = as_right(picks[0] + spread_out[:, :size], 1)
+        tail = jnp.concatenate(picks[1:], axis=0).astype(BF)
+        rows = raw(jnp.concatenate([tail, tail], axis=1), big_ref[...], NN)
+
+        def moved_pick(i, e):
+            if e == 0:
+                return picks[i]
+            return rows[(i - 1) * SLOTS : i * SLOTS, (e - 1) * size : e * size]
+
+        watch = as_right(sum(moved_pick(i, i) for i in range(WINDOW)), 1)
         lefts, rights = [], []
         for l in range(1, WINDOW):
-            shock = picks[l]
-            if l < WINDOW - 1:
-                shock = shock + spread_out[:, l * size : (l + 1) * size]
+            shock = sum(moved_pick(i, i - l) for i in range(l, WINDOW))
             lefts.append(as_left(shock * process, 1))
             rights.append(as_right(shock, 1))
         fixed = raw(
@@ -252,25 +252,14 @@
             ),
             NT,
         )
-        readings = jnp.concatenate(
-            [
-                picks[i] * noise + jnp.where(last_row, -obs_s[pl.ds(step + i, 1), :], 0.0)
-                for i in range(WINDOW)
-            ],
-            axis=1,
-        )
-        every = jnp.concatenate(picks, axis=1).astype(BF)
-        high, low = halves(readings)
-        lowest = (readings - high.astype(F32) - low.astype(F32)).astype(BF)
-        own_noise = raw(
-            jnp.concatenate([high, low, lowest], axis=1),
-            jnp.concatenate([every, every, every], axis=1),
-            NT,
-        )
-        diagonal = (iota((SLOTS, SLOTS), 0) == iota((SLOTS, SLOTS), 1)) & (
-            iota((SLOTS, SLOTS), 0) >= taken
-        )
-        return watch, fixed[:, SLOTS:], fixed[:, :SLOTS] + own_noise + diagonal.astype(F32)
+        readings = sum(picks[i] * obs_s[pl.ds(step + i, 1), :] for i in range(WINDOW))
+        readings = jnp.sum(readings, axis=1, keepdims=True)
+        variances = jnp.sum(sum(picks) * noise, axis=1, keepdims=True)
+        variances = variances + (iota((SLOTS, 1), 0) >= taken).astype(F32)
+        diagonal = iota((SLOTS, SLOTS), 0) == iota((SLOTS, SLOTS), 1)
+        across = jnp.sum(jnp.where(diagonal, readings, 0.0), axis=0, keepdims=True)
+        own_noise = jnp.where(diagonal, variances, 0.0) - jnp.where(last_row, across, 0.0)
+        return watch, fixed[:, SLOTS:], fixed[:, :SLOTS] + own_noise
 
     zero = jnp.int32(0)
     opening = extent(zero, zero)
@@ -293,14 +282,13 @@
             pull_s[...] = jnp.zeros_like(pull_s)
 
         both = as_left(jnp.concatenate([cov_s[...], trans_s[...]], axis=1), 0)
-        watch = watch_s[...]
-        seen = raw(watch, both, NN)
-        seen_cov = jnp.where(last_row, mean_s[...], seen[:, :size])
-        seen_trans = jnp.where(last_row, pull_s[...], seen[:, size:])
-        moving = power(ahead)
-        joint = raw(as_left(seen_cov, 1), jnp.concatenate([watch, moving], axis=0), NT)
-        square = joint[:, :SLOTS] + noise_s[...]
-        side = joint[:, SLOTS:] + fixed_s[...]
+        watch, moving = watch_s[...], power(ahead)
+        both_cov, both_trans = both[:, :size], both[:, size:]
+        seen_cov = jnp.where(last_row, mean_s[...], raw(watch, both_cov, NN))
+        seen_trans = jnp.where(last_row, pull_s[...], raw(watch, both_trans, NN))
+        seen_left = as_left(seen_cov, 1)
+        square = raw(seen_left, watch, NT) + noise_s[...]
+        side = raw(seen_left, moving, NT) + fixed_s[...]
         moved = raw(moving, both, NN)
         moved_cov = raw(as_left(moved[:, :size], 1), moving, NT) + added_ref[ahead]
 
@@ -312,11 +300,11 @@
         mean_s[...] = to_state[SLOTS - 1 :, :]
         pull_s[...] = to_trans[SLOTS - 1 :, :]
         scale = jnp.where(last_row, 0.0, lax.rsqrt(pivots))
-        factors = jnp.concatenate([to_state * scale, to_trans * scale], axis=1)
-        outer = raw(as_left(factors, 0), as_right(factors, 0), TN)
-        cov_s[...] = moved_cov - outer[:size, :size]
-        trans_s[...] = moved[:, size:] - outer[:size, size:]
-        info_s[...] = info_s[...] + outer[size:, size:]
+        gain, reach = to_state * scale, to_trans * scale
+        gain_left, reach_right = as_left(gain, 0), as_right(reach, 0)
+        cov_s[...] = moved_cov - raw(gain_left, as_right(gain, 0), TN)
+        trans_s[...] = moved[:, size:] - raw(gain_left, reach_right, TN)
+        info_s[...] = info_s[...] + raw(as_left(reach, 0), reach_right, TN)
         watch_s[...], fixed_s[...], noise_s[...] = prepared
 
         @pl.when(inside)
@@ -347,12 +335,11 @@
 
 def tables(nw, damping, process_var, obs_var, prior_mean, prior_var):
     size = nw.shape[1]
-    wide = (WINDOW - 1) * size
     return pl.pallas_call(
         tables_kernel,
         out_shape=(
             jax.ShapeDtypeStruct((size, 2 * WINDOW * 3 * size), BF),
-            jax.ShapeDtypeStruct((2 * wide, wide), BF),
+            jax.ShapeDtypeStruct((2 * size, (WINDOW - 1) * size), BF),
             jax.ShapeDtypeStruct((WINDOW + 1, size, size), F32),
             jax.ShapeDtypeStruct((8, size), F32),
         ),

time: 35 us -> 32.5 us (0.929)
  the two profiles are of different devices: /device:TPU:0 before, /device:TPU:26 now
where the time goes in v4:
time: 32.5 us; the launch traced here: 32.2 us
  Pallas kernels  18.1 us (56%)
  waiting for transfers between devices  9.35 us (29%)
  starting transfers between devices  2.56 us (8%)
  other arithmetic  0.79 us (2%)
  local copies, waits for them, and re-layouts  0.74 us (2%)
  between operations  0.69 us (2%)
    pallas_call x1, Pallas kernels, chain(): pl.pallas_call(functools.partial(chain_kernel, own), out_shape=(jax.Shape...  17.5 us
    ppermute x4, waiting for transfers between devices, gather_all(): held = jnp.concatenate([held, lax.ppermute(held, axis, pairs)], axis=0)  9.35 us
    ppermute x4, starting transfers between devices, gather_all(): held = jnp.concatenate([held, lax.ppermute(held, axis, pairs)], axis=0)  2.56 us
    unnamed x14, local copies, waits for them, and re-layouts  0.72 us
    convert_element_type x1, other arithmetic, local(): block = jnp.concatenate([observed, obs_mask.astype(F32)], axis=1)  0.69 us
  transfers between devices with their start and end apart: 4, of which 4 were waited for; matrix products, arithmetic and copies ran while one was open for 0% of the time, Pallas kernels for 2%

profile of v4, /device:TPU:26, one launch (start us, length us, event | category | flops | bytes accessed | tf_op | source)
XLA Modules:
  0.0 32.2 jit_solution(6632119904010766283)
XLA Ops:
  0.6 0.0 copy-start.6
  0.6 0.7 %convert_element_type.3 = f32[2,128]{1,0:T(2,128)S(1)} convert(s32[2,128]{1,0:T(2,128)} %param.9) | non-fusion elementwise | flops 256 | bytes 2048 | tf_op jit(solution)/shard_map/convert_element_type | solution.py:408
  1.3 0.0 copy-done.6
  1.3 0.1 collective-permute-start
  1.4 1.1 %collective-permute-done = f32[2,256]{1,0:T(2,128)S(1)} collective-permute-done((f32[2,256]{1,0:T(2,128)S(1)}, f32[2,256]{1,0:T(2,128)S(1)}, u32[]{:S(2)}, u32[]{:S(2)}) %collective-permute-start) | collective-permute-done | bytes 2080 | tf_op jit(solution)/shard_map/ppermute | solution.py:399
  2.6 1.6 %collective-permute-start.1 = (f32[4,256]{1,0:T(4,128)S(1)}, f32[4,256]{1,0:T(4,128)S(1)}, u32[]{:S(2)}, u32[]{:S(2)}) collective-permute-start(f32[4,256]{1,0:T(4,128)S(1)} %pad_maximum_fusion.2), channel_id=1, source_target_pairs={{0,2},{1,3},{2,0},{3,1},{4,6},{5,7},{6,4},{7,5},{8,10},{9,11},{10,... | collective-permute-start | bytes 12296 | tf_op jit(solution)/shard_map/ppermute | solution.py:399
  4.1 2.1 %collective-permute-done.1 = f32[4,256]{1,0:T(4,128)S(1)} collective-permute-done((f32[4,256]{1,0:T(4,128)S(1)}, f32[4,256]{1,0:T(4,128)S(1)}, u32[]{:S(2)}, u32[]{:S(2)}) %collective-permute-start.1) | collective-permute-done | bytes 4128 | tf_op jit(solution)/shard_map/ppermute | solution.py:399
  6.2 0.5 %collective-permute-start.2 = (f32[8,256]{1,0:T(8,128)S(1)}, f32[8,256]{1,0:T(8,128)S(1)}, u32[]{:S(2)}, u32[]{:S(2)}) collective-permute-start(f32[8,256]{1,0:T(8,128)S(1)} %pad_maximum_fusion.1), channel_id=1, source_target_pairs={{0,4},{1,5},{2,6},{3,7},{4,0},{5,1},{6,2},{7,3},{8,12},{9,13},{10,... | collective-permute-start | bytes 24584 | tf_op jit(solution)/shard_map/ppermute | solution.py:399
  6.8 3.2 %collective-permute-done.2 = f32[8,256]{1,0:T(8,128)S(1)} collective-permute-done((f32[8,256]{1,0:T(8,128)S(1)}, f32[8,256]{1,0:T(8,128)S(1)}, u32[]{:S(2)}, u32[]{:S(2)}) %collective-permute-start.2) | collective-permute-done | bytes 8224 | tf_op jit(solution)/shard_map/ppermute | solution.py:399
  10.0 0.4 %collective-permute-start.3 = (f32[16,256]{1,0:T(8,128)S(1)}, f32[16,256]{1,0:T(8,128)S(1)}, u32[]{:S(2)}, u32[]{:S(2)}) collective-permute-start(f32[16,256]{1,0:T(8,128)S(1)} %pad_maximum_fusion), channel_id=1, source_target_pairs={{0,8},{1,9},{2,10},{3,11},{4,12},{5,13},{6,14},{7,15},{8,0},{9,1},... | collective-permute-start | bytes 49160 | tf_op jit(solution)/shard_map/ppermute | solution.py:399
  10.4 0.1 pad_add_fusion.position_ref
  10.4 0.0 copy-start
  10.4 0.0 copy-start.4
  10.4 0.0 copy-start.5
  10.5 0.0 copy-start.1
  10.5 0.0 copy-start.2
  10.5 0.0 copy-start.3
  10.5 0.7 %copy-done = f32[8,128]{1,0:T(8,128)S(1)} copy-done((f32[8,128]{1,0:T(8,128)S(1)}, f32[8,128]{1,0:T(8,128)}, u32[]{:S(2)}) %copy-start) | copy-done | bytes 4120
  11.1 0.0 copy-done.4
  11.1 0.0 copy-done.5
  11.1 0.0 copy-done.1
  11.1 0.0 copy-done.2
  11.2 0.0 copy-done.3
  11.2 0.6 %shard_map.103 = (bf16[128,3072]{1,0:T(8,128)(2,1)S(1)}, bf16[256,384]{1,0:T(8,128)(2,1)S(1)}, f32[5,128,128]{2,1,0:T(8,128)S(1)}, f32[8,128]{1,0:T(8,128)S(1)}) custom-call(f32[8,128]{1,0:T(8,128)S(1)} %copy-done, f32[1,128]{1,0:T(1,128)S(1)} %bitcast.7, f32[1,128]{1,0:T(1,128)S(1)} %bitcast.8, f32[1,128]{1,0:T(1,128)S(1)} %bitcast.9, ...), custom_call_target="tpu_custom_call" | custom-call | flops 100000000 | bytes 2000000 | tf_op jit(solution)/shard_map/pallas_call | solution.py:338
  11.8 2.9 %collective-permute-done.3 = f32[16,256]{1,0:T(8,128)S(1)} collective-permute-done((f32[16,256]{1,0:T(8,128)S(1)}, f32[16,256]{1,0:T(8,128)S(1)}, u32[]{:S(2)}, u32[]{:S(2)}) %collective-permute-start.3) | collective-permute-done | bytes 16416 | tf_op jit(solution)/shard_map/ppermute | solution.py:399
  14.8 17.5 %shard_map.104 = (f32[2,128]{1,0:T(2,128)}, f32[2,128,128]{2,1,0:T(8,128)}, f32[1,2]{1,0:T(1,128)}) custom-call(s32[2]{0:T(128)S(1)} %pad_add_fusion.position_ref, f32[32,256]{1,0:T(8,128)S(1)} %concatenate.22.gathered_ref, bf16[128,3072]{1,0:T(8,128)(2,1)S(1)} %get-tuple-element.10.strip_ref, bf16[256,384]{1,0:T(8,128)(2,1)S(1)} %get-tuple-element.11.big_ref, ...), custom_call_target="tpu_custom_call" | custom-call | tf_op jit(solution)/shard_map/pallas_call | solution.py:357
  (5 shorter events, 0.1 us)
Async XLA Ops:
  0.6 0.7 %copy-start.6 = (f32[2,128]{1,0:T(2,128)S(1)}, f32[2,128]{1,0:T(2,128)}, u32[]{:S(2)}) copy-start(f32[2,128]{1,0:T(2,128)} %param.8) | copy-start | bytes 3076
  1.3 1.2 %collective-permute-start = (f32[2,256]{1,0:T(2,128)S(1)}, f32[2,256]{1,0:T(2,128)S(1)}, u32[]{:S(2)}, u32[]{:S(2)}) collective-permute-start(f32[2,256]{1,0:T(2,128)S(1)} %pad_maximum_fusion.3), channel_id=1, source_target_pairs={{0,1},{1,0},{2,3},{3,2},{4,5},{5,4},{6,7},{7,6},{8,9},{9,8},{10,11... | collective-permute-start | bytes 6152 | tf_op jit(solution)/shard_map/ppermute | solution.py:399
  2.6 3.7 %collective-permute-start.1 = (f32[4,256]{1,0:T(4,128)S(1)}, f32[4,256]{1,0:T(4,128)S(1)}, u32[]{:S(2)}, u32[]{:S(2)}) collective-permute-start(f32[4,256]{1,0:T(4,128)S(1)} %pad_maximum_fusion.2), channel_id=1, source_target_pairs={{0,2},{1,3},{2,0},{3,1},{4,6},{5,7},{6,4},{7,5},{8,10},{9,11},{10,... | collective-permute-start | bytes 12296 | tf_op jit(solution)/shard_map/ppermute | solution.py:399
  6.2 3.7 %collective-permute-start.2 = (f32[8,256]{1,0:T(8,128)S(1)}, f32[8,256]{1,0:T(8,128)S(1)}, u32[]{:S(2)}, u32[]{:S(2)}) collective-permute-start(f32[8,256]{1,0:T(8,128)S(1)} %pad_maximum_fusion.1), channel_id=1, source_target_pairs={{0,4},{1,5},{2,6},{3,7},{4,0},{5,1},{6,2},{7,3},{8,12},{9,13},{10,... | collective-permute-start | bytes 24584 | tf_op jit(solution)/shard_map/ppermute | solution.py:399
  10.0 4.8 %collective-permute-start.3 = (f32[16,256]{1,0:T(8,128)S(1)}, f32[16,256]{1,0:T(8,128)S(1)}, u32[]{:S(2)}, u32[]{:S(2)}) collective-permute-start(f32[16,256]{1,0:T(8,128)S(1)} %pad_maximum_fusion), channel_id=1, source_target_pairs={{0,8},{1,9},{2,10},{3,11},{4,12},{5,13},{6,14},{7,15},{8,0},{9,1},... | collective-permute-start | bytes 49160 | tf_op jit(solution)/shard_map/ppermute | solution.py:399
  10.4 0.7 %copy-start = (f32[8,128]{1,0:T(8,128)S(1)}, f32[8,128]{1,0:T(8,128)}, u32[]{:S(2)}) copy-start(f32[8,128]{1,0:T(8,128)} %nw_ref.1) | copy-start | bytes 12292
  10.4 0.7 %copy-start.4 = (f32[128]{0:T(128)S(1)}, f32[128]{0:T(128)}, u32[]{:S(2)}) copy-start(f32[128]{0:T(128)} %param.10) | copy-start | bytes 1540
  10.4 0.7 %copy-start.5 = (f32[128]{0:T(128)S(1)}, f32[128]{0:T(128)}, u32[]{:S(2)}) copy-start(f32[128]{0:T(128)} %param.11) | copy-start | bytes 1540
  10.5 0.7 %copy-start.1 = (f32[128]{0:T(128)S(1)}, f32[128]{0:T(128)}, u32[]{:S(2)}) copy-start(f32[128]{0:T(128)} %param.13) | copy-start | bytes 1540
  10.5 0.7 %copy-start.2 = (f32[128]{0:T(128)S(1)}, f32[128]{0:T(128)}, u32[]{:S(2)}) copy-start(f32[128]{0:T(128)} %param.14) | copy-start | bytes 1540
  10.5 0.7 %copy-start.3 = (f32[128]{0:T(128)S(1)}, f32[128]{0:T(128)}, u32[]{:S(2)}) copy-start(f32[128]{0:T(128)} %param.15) | copy-start | bytes 1540

commit v5 on v4

--- a/solution.py
+++ b/solution.py
@@ -13,7 +13,7 @@
 OFFSETS = ((-1, -1), (-1, 0), (-1, 1), (0, -1), (0, 1), (1, -1), (1, 0), (1, 1))
 LOG_TWO_PI = math.log(2.0 * math.pi)
 
-WINDOW = 4
+WINDOW = 5
 SLOTS = 32
 FAR = 1 << 29
 
@@ -67,7 +67,7 @@
 
 def eliminate(square, sides):
     tiles = SLOTS // 8
-    rows = iota((8, 128), 0)
+    rows, lanes = iota((8, 128), 0), iota((8, 128), 1)
     columns = {}
     for k in range(SLOTS - 1):
         for tile in range(k // 8, tiles):
@@ -91,7 +91,7 @@
             if tile == home:
                 scaled = jnp.where(rows > row, scaled, 0.0)
             weights[tile] = scaled
-        quad = quad + weights[tiles - 1] * columns[j, tiles - 1]
+        quad = jnp.where(lanes == j, weights[tiles - 1] * columns[j, tiles - 1], quad)
         for k in range(j + 1, SLOTS - 1):
             across = spread(columns[k, k // 8], row) if k // 8 == home else None
             if across is None:
@@ -99,9 +99,9 @@
             for tile in range(k // 8, tiles):
                 columns[k, tile] = columns[k, tile] - weights[tile] * across
         for part in parts:
-            across = spread(part[home], row)
+            across = jnp.broadcast_to(part[home][row : row + 1, :], part[home].shape)
             for tile in range(home, tiles):
-                part[tile] = part[tile] - weights[tile] * across
+                part[tile] = part[tile] - weights[tile][:, : part[tile].shape[1]] * across
     pivots = jnp.concatenate(pivots, axis=0)
     sides = [jnp.concatenate(part, axis=0) for part in parts]
     return sides, pivots, quad[7:8, :]
@@ -155,7 +155,12 @@
     off_s,
     watch_s,
     fixed_s,
+    square_s,
+    carry_s,
+    cross_s,
     noise_s,
+    next_watch_s,
+    next_fixed_s,
     cov_s,
     trans_s,
     info_s,
@@ -213,7 +218,8 @@
         return (step >= base) & (step < base + own)
 
     def extent(step, first):
-        cut = jnp.where(step < base, base, jnp.where(is_own(step), step + 1, steps))
+        last = base + own - 1
+        cut = jnp.where(step < base, base, jnp.where(step < last, step + 1, steps))
         end = jnp.minimum(step + WINDOW, cut)
         taken = jnp.minimum(off_s[0, end] - first, SLOTS - 1)
         ahead = jnp.int32(0)
@@ -245,13 +251,9 @@
             shock = sum(moved_pick(i, i - l) for i in range(l, WINDOW))
             lefts.append(as_left(shock * process, 1))
             rights.append(as_right(shock, 1))
-        fixed = raw(
-            jnp.concatenate(lefts, axis=1),
-            jnp.concatenate(
-                [jnp.concatenate(rights, axis=1), power(ahead - 1, WINDOW - 1)], axis=0
-            ),
-            NT,
-        )
+        lefts = jnp.concatenate(lefts, axis=1)
+        noise_part = raw(lefts, jnp.concatenate(rights, axis=1), NT)
+        side_part = raw(lefts, power(ahead - 1, WINDOW - 1), NT)
         readings = sum(picks[i] * obs_s[pl.ds(step + i, 1), :] for i in range(WINDOW))
         readings = jnp.sum(readings, axis=1, keepdims=True)
         variances = jnp.sum(sum(picks) * noise, axis=1, keepdims=True)
@@ -259,14 +261,30 @@
         diagonal = iota((SLOTS, SLOTS), 0) == iota((SLOTS, SLOTS), 1)
         across = jnp.sum(jnp.where(diagonal, readings, 0.0), axis=0, keepdims=True)
         own_noise = jnp.where(diagonal, variances, 0.0) - jnp.where(last_row, across, 0.0)
-        return watch, fixed[:, SLOTS:], fixed[:, :SLOTS] + own_noise
+        return watch, side_part, noise_part + own_noise
+
+    def link(ahead, fixed, watch, noise):
+        at = pl.multiple_of((WINDOW - ahead) * band, band)
+        high, low = strip_ref[:, pl.ds(at, size)], strip_ref[:, pl.ds(at + size, size)]
+        rights = [jnp.concatenate([high, high, low], axis=0), as_left(added_ref[ahead], 0)]
+        onward = raw(watch, jnp.concatenate(rights, axis=1), NN)
+        both = raw(as_left(jnp.concatenate([fixed, onward[:, size:]], axis=0), 1), watch, NT)
+        return as_right(onward[:, :size], 1), both[:SLOTS], noise + both[SLOTS:]
 
     zero = jnp.int32(0)
-    opening = extent(zero, zero)
-    watch_s[...], fixed_s[...], noise_s[...] = prepare(zero, zero, *opening)
+    opening = (zero, zero) + extent(zero, zero)
+    second = (opening[3], opening[2])
+    second = second + extent(*second)
+    watch, fixed, noise_now = prepare(*opening)
+    seen = jnp.where(last_row, mean_s[...], raw(watch, as_left(cov_s[...], 0), NN))
+    square_s[...] = raw(as_left(seen, 1), watch, NT) + noise_now
+    watch_s[...], fixed_s[...] = watch, fixed
+    watch, next_fixed, noise_now = prepare(*second)
+    next_watch_s[...], next_fixed_s[...] = watch, next_fixed
+    carry_s[...], cross_s[...], noise_s[...] = link(opening[3], fixed, watch, noise_now)
 
     def body(state):
-        step, first, taken, ahead = state
+        step, first, taken, ahead = state[:4]
         inside = is_own(step)
         mine = jnp.clip(step - base, 0, own - 1)
 
@@ -281,41 +299,57 @@
             info_s[...] = jnp.zeros_like(info_s)
             pull_s[...] = jnp.zeros_like(pull_s)
 
-        both = as_left(jnp.concatenate([cov_s[...], trans_s[...]], axis=1), 0)
-        watch, moving = watch_s[...], power(ahead)
-        both_cov, both_trans = both[:, :size], both[:, size:]
-        seen_cov = jnp.where(last_row, mean_s[...], raw(watch, both_cov, NN))
-        seen_trans = jnp.where(last_row, pull_s[...], raw(watch, both_trans, NN))
-        seen_left = as_left(seen_cov, 1)
-        square = raw(seen_left, watch, NT) + noise_s[...]
-        side = raw(seen_left, moving, NT) + fixed_s[...]
-        moved = raw(moving, both, NN)
-        moved_cov = raw(as_left(moved[:, :size], 1), moving, NT) + added_ref[ahead]
-
-        next_step, next_first = step + ahead, first + taken
-        following = extent(next_step, next_first)
-        prepared = prepare(next_step, next_first, *following)
-
-        (to_state, to_trans), pivots, quad = eliminate(square, (side, seen_trans))
-        mean_s[...] = to_state[SLOTS - 1 :, :]
-        pull_s[...] = to_trans[SLOTS - 1 :, :]
+        square = square_s[...]
+        two = 2 * SLOTS
+        rows = jnp.concatenate([watch_s[...], carry_s[...], power(ahead)], axis=0)
+        seen = raw(rows, as_left(jnp.concatenate([cov_s[...], trans_s[...]], axis=1), 0), NN)
+        seen_cov = jnp.where(last_row, mean_s[...], seen[:SLOTS, :size])
+        seen_trans = jnp.where(last_row, pull_s[...], seen[:SLOTS, size:])
+        lefts = as_left(jnp.concatenate([seen_cov, seen[SLOTS:, :size]], axis=0), 1)
+        joint = raw(lefts[:two], rows[SLOTS:two], NT)
+        cross = joint[:SLOTS] + cross_s[...]
+        next_square = joint[SLOTS:] + noise_s[...]
+        side = raw(lefts[:SLOTS], rows[two:], NT) + fixed_s[...]
+        moved_cov = raw(lefts[two:], rows[two:], NT) + added_ref[ahead]
+        moved_trans = seen[two:, size:]
+
+        after_next = (state[4] + state[7], state[5] + state[6])
+        after_next = after_next + extent(*after_next)
+        new_watch, new_fixed, new_noise = prepare(*after_next)
+        linked = link(state[7], next_fixed_s[...], new_watch, new_noise)
+
+        (cross, to_state, to_trans), pivots, quad = eliminate(square, (cross, side, seen_trans))
         scale = jnp.where(last_row, 0.0, lax.rsqrt(pivots))
+        tie = cross * scale[:, :SLOTS]
+        square_s[...] = (
+            next_square
+            + jnp.where(last_row, cross, 0.0)
+            - raw(as_left(tie, 0), as_right(tie, 0), TN)
+        )
         gain, reach = to_state * scale, to_trans * scale
         gain_left, reach_right = as_left(gain, 0), as_right(reach, 0)
         cov_s[...] = moved_cov - raw(gain_left, as_right(gain, 0), TN)
-        trans_s[...] = moved[:, size:] - raw(gain_left, reach_right, TN)
+        trans_s[...] = moved_trans - raw(gain_left, reach_right, TN)
         info_s[...] = info_s[...] + raw(as_left(reach, 0), reach_right, TN)
-        watch_s[...], fixed_s[...], noise_s[...] = prepared
+        mean_s[...] = to_state[SLOTS - 1 :, :]
+        pull_s[...] = to_trans[SLOTS - 1 :, :]
+        watch_s[...], fixed_s[...] = next_watch_s[...], next_fixed_s[...]
+        next_watch_s[...], next_fixed_s[...] = new_watch, new_fixed
+        carry_s[...], cross_s[...], noise_s[...] = linked
 
         @pl.when(inside)
         def _():
-            log_det = jnp.sum(jnp.log(pivots), axis=0, keepdims=True)
-            count = taken.astype(F32) * LOG_TWO_PI
-            kept_lik[mine] = kept_lik[mine] + (log_det + quad + count)
-
-        return (next_step, next_first) + following
-
-    lax.while_loop(lambda state: state[0] < steps, body, (zero, zero) + opening)
+            counted = jnp.minimum(taken, off_s[0, step + 1] - first)
+            logs = jnp.where(iota((SLOTS, size), 0) < counted, jnp.log(pivots), 0.0)
+            log_det = jnp.sum(logs, axis=0, keepdims=True)
+            squares = jnp.where(iota((1, size), 1) < counted, quad, 0.0)
+            squares = jnp.sum(squares, axis=1, keepdims=True)
+            count = counted.astype(F32) * LOG_TWO_PI
+            kept_lik[mine] = kept_lik[mine] + (log_det + squares + count)
+
+        return state[4:] + after_next
+
+    lax.while_loop(lambda state: state[0] < steps, body, opening + second)
 
     info, pull = info_s[...], pull_s[...]
     for j in range(own - 1, -1, -1):
@@ -372,6 +406,11 @@
             pltpu.VMEM((SLOTS, 3 * size), BF),
             pltpu.VMEM((SLOTS, size), F32),
             pltpu.VMEM((SLOTS, SLOTS), F32),
+            pltpu.VMEM((SLOTS, 3 * size), BF),
+            pltpu.VMEM((SLOTS, SLOTS), F32),
+            pltpu.VMEM((SLOTS, SLOTS), F32),
+            pltpu.VMEM((SLOTS, 3 * size), BF),
+            pltpu.VMEM((SLOTS, size), F32),
             pltpu.VMEM(square, F32),
             pltpu.VMEM(square, F32),
             pltpu.VMEM(square, F32),

time: 32.5 us -> 31.7 us (0.975)
  the two profiles are of different devices: /device:TPU:26 before, /device:TPU:0 now
where the time goes in v5:
time: 31.7 us; the launch traced here: 31.4 us
  Pallas kernels  16.4 us (52%)
  starting transfers between devices  8.66 us (27%)
  waiting for transfers between devices  4.17 us (13%)
  other arithmetic  0.79 us (2%)
  local copies, waits for them, and re-layouts  0.74 us (2%)
  between operations  0.68 us (2%)
    pallas_call x1, Pallas kernels, chain(): pl.pallas_call(functools.partial(chain_kernel, own), out_shape=(jax.Shape...  15.6 us
    ppermute x4, starting transfers between devices, gather_all(): held = jnp.concatenate([held, lax.ppermute(held, axis, pairs)], axis=0)  8.66 us
    ppermute x4, waiting for transfers between devices, gather_all(): held = jnp.concatenate([held, lax.ppermute(held, axis, pairs)], axis=0)  4.17 us
    pallas_call x1, Pallas kernels, tables(): pl.pallas_call(tables_kernel, out_shape=(jax.ShapeDtypeStruct((size, 2 *...  0.78 us
    unnamed x14, local copies, waits for them, and re-layouts  0.72 us
    convert_element_type x1, other arithmetic, local(): block = jnp.concatenate([observed, obs_mask.astype(F32)], axis=1)  0.69 us
  transfers between devices with their start and end apart: 4, of which 4 were waited for; matrix products, arithmetic and copies ran while one was open for 0% of the time, Pallas kernels for 2%

profile of v5, /device:TPU:0, one launch (start us, length us, event | category | flops | bytes accessed | tf_op | source)
XLA Modules:
  0.0 31.4 jit_solution(16016915409316254885)
XLA Ops:
  0.6 0.0 copy-start.6
  0.6 0.7 %convert_element_type.3 = f32[2,128]{1,0:T(2,128)S(1)} convert(s32[2,128]{1,0:T(2,128)} %param.9) | non-fusion elementwise | flops 256 | bytes 2048 | tf_op jit(solution)/shard_map/convert_element_type | solution.py:447
  1.3 0.0 copy-done.6
  1.3 0.5 %collective-permute-start = (f32[2,256]{1,0:T(2,128)S(1)}, f32[2,256]{1,0:T(2,128)S(1)}, u32[]{:S(2)}, u32[]{:S(2)}) collective-permute-start(f32[2,256]{1,0:T(2,128)S(1)} %pad_maximum_fusion.3), channel_id=1, source_target_pairs={{0,1},{1,0},{2,3},{3,2},{4,5},{5,4},{6,7},{7,6},{8,9},{9,8},{10,11... | collective-permute-start | bytes 6152 | tf_op jit(solution)/shard_map/ppermute | solution.py:438
  1.8 0.8 %collective-permute-done = f32[2,256]{1,0:T(2,128)S(1)} collective-permute-done((f32[2,256]{1,0:T(2,128)S(1)}, f32[2,256]{1,0:T(2,128)S(1)}, u32[]{:S(2)}, u32[]{:S(2)}) %collective-permute-start) | collective-permute-done | bytes 2080 | tf_op jit(solution)/shard_map/ppermute | solution.py:438
  2.7 2.9 %collective-permute-start.1 = (f32[4,256]{1,0:T(4,128)S(1)}, f32[4,256]{1,0:T(4,128)S(1)}, u32[]{:S(2)}, u32[]{:S(2)}) collective-permute-start(f32[4,256]{1,0:T(4,128)S(1)} %pad_maximum_fusion.2), channel_id=1, source_target_pairs={{0,2},{1,3},{2,0},{3,1},{4,6},{5,7},{6,4},{7,5},{8,10},{9,11},{10,... | collective-permute-start | bytes 12296 | tf_op jit(solution)/shard_map/ppermute | solution.py:438
  5.6 1.6 %collective-permute-done.1 = f32[4,256]{1,0:T(4,128)S(1)} collective-permute-done((f32[4,256]{1,0:T(4,128)S(1)}, f32[4,256]{1,0:T(4,128)S(1)}, u32[]{:S(2)}, u32[]{:S(2)}) %collective-permute-start.1) | collective-permute-done | bytes 4128 | tf_op jit(solution)/shard_map/ppermute | solution.py:438
  7.2 2.1 %collective-permute-start.2 = (f32[8,256]{1,0:T(8,128)S(1)}, f32[8,256]{1,0:T(8,128)S(1)}, u32[]{:S(2)}, u32[]{:S(2)}) collective-permute-start(f32[8,256]{1,0:T(8,128)S(1)} %pad_maximum_fusion.1), channel_id=1, source_target_pairs={{0,4},{1,5},{2,6},{3,7},{4,0},{5,1},{6,2},{7,3},{8,12},{9,13},{10,... | collective-permute-start | bytes 24584 | tf_op jit(solution)/shard_map/ppermute | solution.py:438
  9.3 1.6 %collective-permute-done.2 = f32[8,256]{1,0:T(8,128)S(1)} collective-permute-done((f32[8,256]{1,0:T(8,128)S(1)}, f32[8,256]{1,0:T(8,128)S(1)}, u32[]{:S(2)}, u32[]{:S(2)}) %collective-permute-start.2) | collective-permute-done | bytes 8224 | tf_op jit(solution)/shard_map/ppermute | solution.py:438
  11.0 3.1 %collective-permute-start.3 = (f32[16,256]{1,0:T(8,128)S(1)}, f32[16,256]{1,0:T(8,128)S(1)}, u32[]{:S(2)}, u32[]{:S(2)}) collective-permute-start(f32[16,256]{1,0:T(8,128)S(1)} %pad_maximum_fusion), channel_id=1, source_target_pairs={{0,8},{1,9},{2,10},{3,11},{4,12},{5,13},{6,14},{7,15},{8,0},{9,1},... | collective-permute-start | bytes 49160 | tf_op jit(solution)/shard_map/ppermute | solution.py:438
  14.1 0.1 pad_add_fusion.position_ref
  14.1 0.0 copy-start
  14.1 0.0 copy-start.4
  14.2 0.0 copy-start.5
  14.2 0.0 copy-start.1
  14.2 0.0 copy-start.2
  14.2 0.0 copy-start.3
  14.2 0.7 %copy-done = f32[8,128]{1,0:T(8,128)S(1)} copy-done((f32[8,128]{1,0:T(8,128)S(1)}, f32[8,128]{1,0:T(8,128)}, u32[]{:S(2)}) %copy-start) | copy-done | bytes 4120
  14.8 0.0 copy-done.4
  14.8 0.0 copy-done.5
  14.8 0.0 copy-done.1
  14.8 0.0 copy-done.2
  14.9 0.0 copy-done.3
  14.9 0.8 %shard_map.103 = (bf16[128,3840]{1,0:T(8,128)(2,1)S(1)}, bf16[256,512]{1,0:T(8,128)(2,1)S(1)}, f32[6,128,128]{2,1,0:T(8,128)S(1)}, f32[8,128]{1,0:T(8,128)S(1)}) custom-call(f32[8,128]{1,0:T(8,128)S(1)} %copy-done, f32[1,128]{1,0:T(1,128)S(1)} %bitcast.7, f32[1,128]{1,0:T(1,128)S(1)} %bitcast.8, f32[1,128]{1,0:T(1,128)S(1)} %bitcast.9, ...), custom_call_target="tpu_custom_call" | custom-call | flops 100000000 | bytes 2000000 | tf_op jit(solution)/shard_map/pallas_call | solution.py:372
  15.7 0.1 collective-permute-done.3
  15.8 15.6 %shard_map.104 = (f32[2,128]{1,0:T(2,128)}, f32[2,128,128]{2,1,0:T(8,128)}, f32[1,2]{1,0:T(1,128)}) custom-call(s32[2]{0:T(128)S(1)} %pad_add_fusion.position_ref, f32[32,256]{1,0:T(8,128)S(1)} %concatenate.22.gathered_ref, bf16[128,3840]{1,0:T(8,128)(2,1)S(1)} %get-tuple-element.10.strip_ref, bf16[256,512]{1,0:T(8,128)(2,1)S(1)} %get-tuple-element.11.big_ref, ...), custom_call_target="tpu_custom_call" | custom-call | tf_op jit(solution)/shard_map/pallas_call | solution.py:391
  (5 shorter events, 0.1 us)
Async XLA Ops:
  0.6 0.7 %copy-start.6 = (f32[2,128]{1,0:T(2,128)S(1)}, f32[2,128]{1,0:T(2,128)}, u32[]{:S(2)}) copy-start(f32[2,128]{1,0:T(2,128)} %param.8) | copy-start | bytes 3076
  1.3 1.3 %collective-permute-start = (f32[2,256]{1,0:T(2,128)S(1)}, f32[2,256]{1,0:T(2,128)S(1)}, u32[]{:S(2)}, u32[]{:S(2)}) collective-permute-start(f32[2,256]{1,0:T(2,128)S(1)} %pad_maximum_fusion.3), channel_id=1, source_target_pairs={{0,1},{1,0},{2,3},{3,2},{4,5},{5,4},{6,7},{7,6},{8,9},{9,8},{10,11... | collective-permute-start | bytes 6152 | tf_op jit(solution)/shard_map/ppermute | solution.py:438
  2.7 4.5 %collective-permute-start.1 = (f32[4,256]{1,0:T(4,128)S(1)}, f32[4,256]{1,0:T(4,128)S(1)}, u32[]{:S(2)}, u32[]{:S(2)}) collective-permute-start(f32[4,256]{1,0:T(4,128)S(1)} %pad_maximum_fusion.2), channel_id=1, source_target_pairs={{0,2},{1,3},{2,0},{3,1},{4,6},{5,7},{6,4},{7,5},{8,10},{9,11},{10,... | collective-permute-start | bytes 12296 | tf_op jit(solution)/shard_map/ppermute | solution.py:438
  7.2 3.8 %collective-permute-start.2 = (f32[8,256]{1,0:T(8,128)S(1)}, f32[8,256]{1,0:T(8,128)S(1)}, u32[]{:S(2)}, u32[]{:S(2)}) collective-permute-start(f32[8,256]{1,0:T(8,128)S(1)} %pad_maximum_fusion.1), channel_id=1, source_target_pairs={{0,4},{1,5},{2,6},{3,7},{4,0},{5,1},{6,2},{7,3},{8,12},{9,13},{10,... | collective-permute-start | bytes 24584 | tf_op jit(solution)/shard_map/ppermute | solution.py:438
  11.0 4.8 %collective-permute-start.3 = (f32[16,256]{1,0:T(8,128)S(1)}, f32[16,256]{1,0:T(8,128)S(1)}, u32[]{:S(2)}, u32[]{:S(2)}) collective-permute-start(f32[16,256]{1,0:T(8,128)S(1)} %pad_maximum_fusion), channel_id=1, source_target_pairs={{0,8},{1,9},{2,10},{3,11},{4,12},{5,13},{6,14},{7,15},{8,0},{9,1},... | collective-permute-start | bytes 49160 | tf_op jit(solution)/shard_map/ppermute | solution.py:438
  14.1 0.7 %copy-start = (f32[8,128]{1,0:T(8,128)S(1)}, f32[8,128]{1,0:T(8,128)}, u32[]{:S(2)}) copy-start(f32[8,128]{1,0:T(8,128)} %nw_ref.1) | copy-start | bytes 12292
  14.1 0.7 %copy-start.4 = (f32[128]{0:T(128)S(1)}, f32[128]{0:T(128)}, u32[]{:S(2)}) copy-start(f32[128]{0:T(128)} %param.10) | copy-start | bytes 1540
  14.2 0.7 %copy-start.5 = (f32[128]{0:T(128)S(1)}, f32[128]{0:T(128)}, u32[]{:S(2)}) copy-start(f32[128]{0:T(128)} %param.11) | copy-start | bytes 1540
  14.2 0.7 %copy-start.1 = (f32[128]{0:T(128)S(1)}, f32[128]{0:T(128)}, u32[]{:S(2)}) copy-start(f32[128]{0:T(128)} %param.13) | copy-start | bytes 1540
  14.2 0.7 %copy-start.2 = (f32[128]{0:T(128)S(1)}, f32[128]{0:T(128)}, u32[]{:S(2)}) copy-start(f32[128]{0:T(128)} %param.14) | copy-start | bytes 1540
  14.2 0.7 %copy-start.3 = (f32[128]{0:T(128)S(1)}, f32[128]{0:T(128)}, u32[]{:S(2)}) copy-start(f32[128]{0:T(128)} %param.15) | copy-start | bytes 1540
